TPU v7x, 128 devices: a whole 4x4x4 slice. The times are simulated.
128 devices in a mesh: dp: 4 (over y), ctx: 32 (over x, z, core).
Axes of the slice: x: 4, y: 4, z: 4, core: 2. Of those that a mesh axis runs over, the one named last changes fastest.
Arguments:
- tokens: bfloat16 [16384, 576], P(('dp', 'ctx')), may hold values from -6 to 6
- out_grad: bfloat16 [16384, 576], P(('dp', 'ctx')), may hold values from -6 to 6
- w_query: bfloat16 [2, 576, 576], P(None, 'dp'), may hold values from -0.25 to 0.25
- w_key: bfloat16 [2, 576, 192], P(None, 'dp'), may hold values from -0.25 to 0.25
- w_value: bfloat16 [2, 576, 192], P(None, 'dp'), may hold values from -0.25 to 0.25
- w_out: bfloat16 [2, 576, 576], P(None, 'dp'), may hold values from -2 to 2
- w_gate: bfloat16 [2, 576, 1536], P(None, 'dp'), may hold values from -0.25 to 0.25
- w_up: bfloat16 [2, 576, 1536], P(None, 'dp'), may hold values from -0.25 to 0.25
- w_down: bfloat16 [2, 1536, 576], P(None, 'dp'), may hold values from -0.15625 to 0.15625
- attn_gain: bfloat16 [2, 576], P(None, 'dp'), may hold values from 0.5 to 1.5
- ffn_gain: bfloat16 [2, 576], P(None, 'dp'), may hold values from 0.5 to 1.5
- block_pairs: int32 [32], replicated, may hold values from 0 to 31, each once
Outputs:
- out: bfloat16 [16384, 576], P(('dp', 'ctx'))
- tokens_grad: float32 [16384, 576], P(('dp', 'ctx'))
- grad_query: float32 [2, 576, 576], P(None, 'dp')
- grad_key: float32 [2, 576, 192], P(None, 'dp')
- grad_value: float32 [2, 576, 192], P(None, 'dp')
- grad_out: float32 [2, 576, 576], P(None, 'dp')
- grad_gate: float32 [2, 576, 1536], P(None, 'dp')
- grad_up: float32 [2, 576, 1536], P(None, 'dp')
- grad_down: float32 [2, 1536, 576], P(None, 'dp')
- grad_attn_gain: float32 [2, 576], P(None, 'dp')
- grad_ffn_gain: float32 [2, 576], P(None, 'dp')
Inputs may be any that keep to these rules, and one draw needn't show every extreme that they name: A permutation of the ctx indices; ctx index c holds blocks block_pairs[c] and 63 - block_pairs[c] of each of its sequences.
All inputs are finite; a program needn't handle non-finite values.
Results may differ from a plain program's by a relative error of at most 0.03.
Values may be sent and summed in bfloat16 or wider, within the bound.
A program may use at most 128 MiB of HBM per device.

v0:
```python
import jax
import jax.numpy as jnp
from jax import lax
from jax.sharding import PartitionSpec as P

HEADS = 9
KV_HEADS = 3
HEAD_DIM = 64
LAYERS = 2


NORM_EPS = 1e-05
ROPE_BASE = 100000.0
NEG_BIG = -1e30


def rms_norm(hidden, gain_vec):
    inv_rms = lax.rsqrt(jnp.mean(hidden * hidden, axis=-1, keepdims=True) + NORM_EPS)
    return hidden * inv_rms * gain_vec


def rope_tables(positions, head_width):
    half_width = head_width // 2
    frequency = ROPE_BASE ** (-2.0 * jnp.arange(half_width, dtype=jnp.float32) / head_width)
    angles = positions.astype(jnp.float32)[:, None] * frequency[None, :]
    angles = jnp.concatenate([angles, angles], axis=1)
    return (jnp.cos(angles), jnp.sin(angles))


def rotate(heads_in, cosine_table, sine_table):
    half_width = heads_in.shape[-1] // 2
    turned = jnp.concatenate([-heads_in[..., half_width:], heads_in[..., :half_width]], axis=-1)
    return heads_in * cosine_table[:, None, :] + turned * sine_table[:, None, :]


def slot_positions(block_pairs, device_idx, half_rows, ctx_count):
    first_block = block_pairs[device_idx]
    second_block = 2 * ctx_count - 1 - first_block
    offsets = jnp.arange(half_rows, dtype=jnp.int32)
    return jnp.concatenate([first_block * half_rows + offsets, second_block * half_rows + offsets])


def masked_scores(queries, key_block, query_pos, key_pos):
    scores = jnp.einsum("tkgd,skd->kgts", queries, key_block, preferred_element_type=jnp.float32)
    visible = key_pos[None, None, None, :] <= query_pos[None, None, :, None]
    return jnp.where(visible, scores, NEG_BIG)


def split_block(kv_block):
    kv_width = KV_HEADS * HEAD_DIM
    block_len = kv_block.shape[0]
    key_block = kv_block[:, :kv_width].reshape(block_len, KV_HEADS, HEAD_DIM)
    value_block = kv_block[:, kv_width:].reshape(block_len, KV_HEADS, HEAD_DIM)
    return (key_block, value_block)


def key_blocks(all_kv, key_pos):
    seq_len = all_kv.shape[0]
    block_len = min(512, seq_len)
    block_count = seq_len // block_len
    return (
        all_kv.reshape(block_count, block_len, all_kv.shape[1]),
        key_pos.reshape(block_count, block_len),
    )


def layer_forward(hidden, params, query_pos, key_pos, cosine_table, sine_table):
    query_w, key_w, value_w, out_w, gate_w, up_w, down_w, gain_attn, gain_ffn = params
    row_count = hidden.shape[0]
    kv_width = KV_HEADS * HEAD_DIM
    group_size = HEADS // KV_HEADS
    normed = rms_norm(hidden, gain_attn.astype(jnp.float32)).astype(jnp.bfloat16)
    q_raw = jnp.dot(normed, query_w, preferred_element_type=jnp.float32).reshape(
        row_count, HEADS, HEAD_DIM
    )
    k_raw = jnp.dot(normed, key_w, preferred_element_type=jnp.float32).reshape(
        row_count, KV_HEADS, HEAD_DIM
    )
    v_raw = jnp.dot(normed, value_w, preferred_element_type=jnp.float32)
    queries = (rotate(q_raw, cosine_table, sine_table) * 0.125).astype(jnp.bfloat16)
    queries = queries.reshape(row_count, KV_HEADS, group_size, HEAD_DIM)
    key_rows = (
        rotate(k_raw, cosine_table, sine_table).astype(jnp.bfloat16).reshape(row_count, kv_width)
    )
    local_kv = jnp.concatenate([key_rows, v_raw.astype(jnp.bfloat16)], axis=1)
    all_kv = lax.all_gather(local_kv, "ctx", axis=0, tiled=True)
    kv_stack, pos_stack = key_blocks(all_kv, key_pos)

    def stats_step(carry, inputs):
        running_max, running_sum = carry
        kv_block, block_pos = inputs
        key_block, value_block = split_block(kv_block)
        scores = masked_scores(queries, key_block, query_pos, block_pos)
        new_max = jnp.maximum(running_max, jnp.max(scores, axis=-1))
        running_sum = running_sum * jnp.exp(running_max - new_max) + jnp.sum(
            jnp.exp(scores - new_max[..., None]), axis=-1
        )
        return ((new_max, running_sum), None)

    start_max = jnp.full((KV_HEADS, group_size, row_count), NEG_BIG, jnp.float32)
    (running_max, running_sum), ignored = lax.scan(
        stats_step, (start_max, jnp.zeros_like(start_max)), (kv_stack, pos_stack)
    )
    log_total = running_max + jnp.log(running_sum)

    def value_step(accumulated, inputs):
        kv_block, block_pos = inputs
        key_block, value_block = split_block(kv_block)
        attn_probs = jnp.exp(
            masked_scores(queries, key_block, query_pos, block_pos) - log_total[..., None]
        )
        update = jnp.einsum(
            "kgts,skd->tkgd",
            attn_probs.astype(jnp.bfloat16),
            value_block,
            preferred_element_type=jnp.float32,
        )
        return (accumulated + update, None)

    start_acc = jnp.zeros((row_count, KV_HEADS, group_size, HEAD_DIM), jnp.float32)
    attn_full, ignored = lax.scan(value_step, start_acc, (kv_stack, pos_stack))
    attn_low = attn_full.reshape(row_count, HEADS * HEAD_DIM).astype(jnp.bfloat16)
    mid_hidden = hidden + jnp.dot(attn_low, out_w, preferred_element_type=jnp.float32)
    normed_ffn = rms_norm(mid_hidden, gain_ffn.astype(jnp.float32)).astype(jnp.bfloat16)
    gate = jnp.dot(normed_ffn, gate_w, preferred_element_type=jnp.float32)
    up_proj = jnp.dot(normed_ffn, up_w, preferred_element_type=jnp.float32)
    inner = (jax.nn.silu(gate) * up_proj).astype(jnp.bfloat16)
    new_hidden = mid_hidden + jnp.dot(inner, down_w, preferred_element_type=jnp.float32)
    saved_state = (
        hidden,
        normed,
        q_raw,
        k_raw,
        queries,
        all_kv,
        log_total,
        attn_full,
        attn_low,
        mid_hidden,
        normed_ffn,
        gate,
        up_proj,
        inner,
    )
    return (new_hidden, saved_state)


def layer_backward(grad_hidden, params, saved_state, query_pos, key_pos, cosine_table, sine_table):
    query_w, key_w, value_w, out_w, gate_w, up_w, down_w, gain_attn, gain_ffn = params
    (
        hidden,
        normed,
        q_raw,
        k_raw,
        queries,
        all_kv,
        log_total,
        attn_full,
        attn_low,
        mid_hidden,
        normed_ffn,
        gate,
        up_proj,
        inner,
    ) = saved_state
    row_count = hidden.shape[0]
    kv_width = KV_HEADS * HEAD_DIM
    group_size = HEADS // KV_HEADS
    ffn_grad = grad_hidden.astype(jnp.bfloat16)
    grad_down = jnp.dot(inner.T, ffn_grad, preferred_element_type=jnp.float32)
    grad_inner = jnp.dot(ffn_grad, down_w.T, preferred_element_type=jnp.float32)
    ignored, swiglu_back = jax.vjp(
        lambda gate_in, up_in: jax.nn.silu(gate_in) * up_in, gate, up_proj
    )
    grad_gate_act, grad_up_act = swiglu_back(grad_inner)
    grad_gate_act = grad_gate_act.astype(jnp.bfloat16)
    grad_up_act = grad_up_act.astype(jnp.bfloat16)
    grad_gate = jnp.dot(normed_ffn.T, grad_gate_act, preferred_element_type=jnp.float32)
    grad_up = jnp.dot(normed_ffn.T, grad_up_act, preferred_element_type=jnp.float32)
    grad_normed_ffn = jnp.dot(
        grad_gate_act, gate_w.T, preferred_element_type=jnp.float32
    ) + jnp.dot(grad_up_act, up_w.T, preferred_element_type=jnp.float32)
    ignored, norm_back_ffn = jax.vjp(rms_norm, mid_hidden, gain_ffn.astype(jnp.float32))
    grad_mid, grad_gain_ffn = norm_back_ffn(grad_normed_ffn)
    grad_mid = grad_mid + grad_hidden
    attn_grad = grad_mid.astype(jnp.bfloat16)
    grad_out = jnp.dot(attn_low.T, attn_grad, preferred_element_type=jnp.float32)
    grad_attn = jnp.dot(attn_grad, out_w.T, preferred_element_type=jnp.float32).astype(jnp.bfloat16)
    grad_attn = grad_attn.reshape(row_count, KV_HEADS, group_size, HEAD_DIM)
    delta = jnp.einsum("tkgd,tkgd->kgt", grad_attn.astype(jnp.float32), attn_full)
    kv_stack, pos_stack = key_blocks(all_kv, key_pos)

    def grad_step(query_acc, inputs):
        kv_block, block_pos = inputs
        key_block, value_block = split_block(kv_block)
        block_len = kv_block.shape[0]
        attn_probs = jnp.exp(
            masked_scores(queries, key_block, query_pos, block_pos) - log_total[..., None]
        )
        grad_probs = jnp.einsum(
            "tkgd,skd->kgts", grad_attn, value_block, preferred_element_type=jnp.float32
        )
        grad_scores = (attn_probs * (grad_probs - delta[..., None])).astype(jnp.bfloat16)
        query_acc = query_acc + jnp.einsum(
            "kgts,skd->tkgd", grad_scores, key_block, preferred_element_type=jnp.float32
        )
        grad_keys = jnp.einsum(
            "kgts,tkgd->skd", grad_scores, queries, preferred_element_type=jnp.float32
        )
        grad_values = jnp.einsum(
            "kgts,tkgd->skd",
            attn_probs.astype(jnp.bfloat16),
            grad_attn,
            preferred_element_type=jnp.float32,
        )
        stacked = jnp.concatenate(
            [grad_keys.reshape(block_len, kv_width), grad_values.reshape(block_len, kv_width)],
            axis=1,
        )
        return (query_acc, stacked)

    start_acc = jnp.zeros((row_count, KV_HEADS, group_size, HEAD_DIM), jnp.float32)
    query_acc, kv_terms = lax.scan(grad_step, start_acc, (kv_stack, pos_stack))
    kv_terms = kv_terms.reshape(all_kv.shape[0], 2 * kv_width)
    kv_grads = lax.psum_scatter(
        kv_terms.astype(jnp.bfloat16), "ctx", scatter_dimension=0, tiled=True
    ).astype(jnp.float32)
    ignored, query_back = jax.vjp(
        lambda heads_in: rotate(heads_in, cosine_table, sine_table) * 0.125, q_raw
    )
    grad_q_raw = query_back(query_acc.reshape(row_count, HEADS, HEAD_DIM))[0]
    grad_q_raw = grad_q_raw.astype(jnp.bfloat16).reshape(row_count, HEADS * HEAD_DIM)
    ignored, key_back = jax.vjp(lambda heads_in: rotate(heads_in, cosine_table, sine_table), k_raw)
    grad_k_raw = key_back(kv_grads[:, :kv_width].reshape(row_count, KV_HEADS, HEAD_DIM))[0]
    grad_k_raw = grad_k_raw.astype(jnp.bfloat16).reshape(row_count, kv_width)
    grad_v_raw = kv_grads[:, kv_width:].astype(jnp.bfloat16)
    grad_query = jnp.dot(normed.T, grad_q_raw, preferred_element_type=jnp.float32)
    grad_key = jnp.dot(normed.T, grad_k_raw, preferred_element_type=jnp.float32)
    grad_value = jnp.dot(normed.T, grad_v_raw, preferred_element_type=jnp.float32)
    grad_normed = (
        jnp.dot(grad_q_raw, query_w.T, preferred_element_type=jnp.float32)
        + jnp.dot(grad_k_raw, key_w.T, preferred_element_type=jnp.float32)
        + jnp.dot(grad_v_raw, value_w.T, preferred_element_type=jnp.float32)
    )
    ignored, norm_back_attn = jax.vjp(rms_norm, hidden, gain_attn.astype(jnp.float32))
    grad_input, grad_gain_attn = norm_back_attn(grad_normed)
    layer_grads = (
        grad_query,
        grad_key,
        grad_value,
        grad_out,
        grad_gate,
        grad_up,
        grad_down,
        grad_gain_attn,
        grad_gain_ffn,
    )
    return (grad_input + grad_mid, layer_grads)


def body(
    tokens,
    out_grad,
    w_query,
    w_key,
    w_value,
    w_out,
    w_gate,
    w_up,
    w_down,
    attn_gain,
    ffn_gain,
    block_pairs,
):
    ctx_count = lax.axis_size("ctx")
    ctx_index = lax.axis_index("ctx")
    row_count = tokens.shape[0]
    half_rows = row_count // 2
    query_pos = slot_positions(block_pairs, ctx_index, half_rows, ctx_count)
    key_pos = jax.vmap(
        lambda device_idx: slot_positions(block_pairs, device_idx, half_rows, ctx_count)
    )(jnp.arange(ctx_count, dtype=jnp.int32)).reshape(-1)
    cosine_table, sine_table = rope_tables(query_pos, HEAD_DIM)
    hidden = tokens.astype(jnp.float32)
    kept_params = []
    kept_states = []
    for layer_idx in range(LAYERS):
        params = (
            lax.all_gather(w_query[layer_idx], "dp", axis=0, tiled=True),
            lax.all_gather(w_key[layer_idx], "dp", axis=0, tiled=True),
            lax.all_gather(w_value[layer_idx], "dp", axis=0, tiled=True),
            lax.all_gather(w_out[layer_idx], "dp", axis=0, tiled=True),
            lax.all_gather(w_gate[layer_idx], "dp", axis=0, tiled=True),
            lax.all_gather(w_up[layer_idx], "dp", axis=0, tiled=True),
            lax.all_gather(w_down[layer_idx], "dp", axis=0, tiled=True),
            lax.all_gather(attn_gain[layer_idx], "dp", axis=0, tiled=True),
            lax.all_gather(ffn_gain[layer_idx], "dp", axis=0, tiled=True),
        )
        hidden, saved_state = layer_forward(
            hidden, params, query_pos, key_pos, cosine_table, sine_table
        )
        kept_params.append(params)
        kept_states.append(saved_state)
    result = hidden.astype(jnp.bfloat16)
    grad_hidden = out_grad.astype(jnp.float32)
    grads_by_layer = [None] * LAYERS
    for layer_idx in reversed(range(LAYERS)):
        params = (
            lax.all_gather(w_query[layer_idx], "dp", axis=0, tiled=True),
            lax.all_gather(w_key[layer_idx], "dp", axis=0, tiled=True),
            lax.all_gather(w_value[layer_idx], "dp", axis=0, tiled=True),
            lax.all_gather(w_out[layer_idx], "dp", axis=0, tiled=True),
            lax.all_gather(w_gate[layer_idx], "dp", axis=0, tiled=True),
            lax.all_gather(w_up[layer_idx], "dp", axis=0, tiled=True),
            lax.all_gather(w_down[layer_idx], "dp", axis=0, tiled=True),
            lax.all_gather(attn_gain[layer_idx], "dp", axis=0, tiled=True),
            lax.all_gather(ffn_gain[layer_idx], "dp", axis=0, tiled=True),
        )
        grad_hidden, layer_grads = layer_backward(
            grad_hidden,
            params,
            kept_states[layer_idx],
            query_pos,
            key_pos,
            cosine_table,
            sine_table,
        )
        (
            grad_query,
            grad_key,
            grad_value,
            grad_out,
            grad_gate,
            grad_up,
            grad_down,
            grad_gain_attn,
            grad_gain_ffn,
        ) = layer_grads
        shard_grads = (
            lax.psum_scatter(
                grad_query.astype(jnp.bfloat16), "dp", scatter_dimension=0, tiled=True
            ).astype(jnp.float32),
            lax.psum_scatter(
                grad_key.astype(jnp.bfloat16), "dp", scatter_dimension=0, tiled=True
            ).astype(jnp.float32),
            lax.psum_scatter(
                grad_value.astype(jnp.bfloat16), "dp", scatter_dimension=0, tiled=True
            ).astype(jnp.float32),
            lax.psum_scatter(
                grad_out.astype(jnp.bfloat16), "dp", scatter_dimension=0, tiled=True
            ).astype(jnp.float32),
            lax.psum_scatter(
                grad_gate.astype(jnp.bfloat16), "dp", scatter_dimension=0, tiled=True
            ).astype(jnp.float32),
            lax.psum_scatter(
                grad_up.astype(jnp.bfloat16), "dp", scatter_dimension=0, tiled=True
            ).astype(jnp.float32),
            lax.psum_scatter(
                grad_down.astype(jnp.bfloat16), "dp", scatter_dimension=0, tiled=True
            ).astype(jnp.float32),
            lax.psum_scatter(
                grad_gain_attn.astype(jnp.bfloat16), "dp", scatter_dimension=0, tiled=True
            ).astype(jnp.float32),
            lax.psum_scatter(
                grad_gain_ffn.astype(jnp.bfloat16), "dp", scatter_dimension=0, tiled=True
            ).astype(jnp.float32),
        )
        shard_grads = (
            lax.psum(shard_grads[0].astype(jnp.bfloat16), "ctx").astype(jnp.float32),
            lax.psum(shard_grads[1].astype(jnp.bfloat16), "ctx").astype(jnp.float32),
            lax.psum(shard_grads[2].astype(jnp.bfloat16), "ctx").astype(jnp.float32),
            lax.psum(shard_grads[3].astype(jnp.bfloat16), "ctx").astype(jnp.float32),
            lax.psum(shard_grads[4].astype(jnp.bfloat16), "ctx").astype(jnp.float32),
            lax.psum(shard_grads[5].astype(jnp.bfloat16), "ctx").astype(jnp.float32),
            lax.psum(shard_grads[6].astype(jnp.bfloat16), "ctx").astype(jnp.float32),
            lax.psum(shard_grads[7].astype(jnp.bfloat16), "ctx").astype(jnp.float32),
            lax.psum(shard_grads[8].astype(jnp.bfloat16), "ctx").astype(jnp.float32),
        )
        grads_by_layer[layer_idx] = shard_grads
    stacked = [
        jnp.stack([grads_by_layer[layer_idx][item_idx] for layer_idx in range(LAYERS)])
        for item_idx in range(9)
    ]
    return (
        result,
        grad_hidden,
        stacked[0],
        stacked[1],
        stacked[2],
        stacked[3],
        stacked[4],
        stacked[5],
        stacked[6],
        stacked[7],
        stacked[8],
    )


def solution(mesh):
    in_specs = (
        P(("dp", "ctx"), None),
        P(("dp", "ctx"), None),
        P(None, "dp", None),
        P(None, "dp", None),
        P(None, "dp", None),
        P(None, "dp", None),
        P(None, "dp", None),
        P(None, "dp", None),
        P(None, "dp", None),
        P(None, "dp"),
        P(None, "dp"),
        P(),
    )
    out_specs = (
        P(("dp", "ctx"), None),
        P(("dp", "ctx"), None),
        P(None, "dp", None),
        P(None, "dp", None),
        P(None, "dp", None),
        P(None, "dp", None),
        P(None, "dp", None),
        P(None, "dp", None),
        P(None, "dp", None),
        P(None, "dp"),
        P(None, "dp"),
    )
    return jax.shard_map(body, mesh=mesh, in_specs=in_specs, out_specs=out_specs, check_vma=False)
```

profile of v0, /device:TPU:1, one launch (start us, length us, event | category | flops | bytes accessed | tf_op | source)
XLA Modules:
  0.0 1323.9 jit_solution(6938909658842467629)
XLA Ops:
  110.3 30.9 %while.74 = (s32[]{:T(128)}, f32[3,3,128]{2,1,0:T(4,128)S(1)}, f32[3,3,128]{2,1,0:T(4,128)S(1)}, s32[8,512]{1,0:T(8,128)}, s32[128]{0:T(128)S(1)}, /*index=5*/bf...) while((s32[]{:T(128)}, f32[3,3,128]{2,1,0:T(4,128)S(1)}, ...), condition=%wide.region_4.5_spmd.clone, body=%wide.region_1.4_spmd.clone.sunk | while | flops 78517888 | bytes 6505592 | solution.py:101
  141.2 35.8 %while.75 = (s32[]{:T(128)}, f32[128,3,3,64]{0,3,2,1:T(8,128)}, bf16[8,512,384]{1,2,0:T(8,128)(2,1)}, s32[8,512]{1,0:T(8,128)}, s32[128]{0:T(128)S(1)}, /*index=...) while((s32[]{:T(128)}, f32[128,3,3,64]{0,3,2,1:T(8,128)}, ...), condition=%wide.region_6.7_spmd.clone, body=%wide.region_5.6_spmd.clone.sunk | while | flops 152977408 | bytes 2845815 | solution.py:121
  237.8 45.2 %all-gather.29.cloned.1.call-done = bf16[4096,384]{0,1:T(8,128)(2,1)} async-done(((bf16[128,384]{0,1:T(8,128)(2,1)}), bf16[4096,384]{0,1:T(8,128)(2,1)}) %all-gather.29.cloned.1.call-update) | async-done | bytes 3145744 | tf_op jit(solution)/shard_map/all_gather | solution.py:86
  286.8 30.9 %while.76 = (s32[]{:T(128)}, f32[3,3,128]{2,1,0:T(4,128)S(1)}, f32[3,3,128]{2,1,0:T(4,128)S(1)}, s32[8,512]{1,0:T(8,128)}, s32[128]{0:T(128)S(1)}, /*index=5*/bf...) while((s32[]{:T(128)}, f32[3,3,128]{2,1,0:T(4,128)S(1)}, ...), condition=%wide.region_12.13_spmd.clone, body=%wide.region_9.12_spmd.clone.sunk | while | flops 78517888 | bytes 6505592 | solution.py:101
  318.4 35.9 %while.77 = (s32[]{:T(128)}, f32[128,3,3,64]{0,3,2,1:T(8,128)}, bf16[8,512,384]{1,2,0:T(8,128)(2,1)}, s32[8,512]{1,0:T(8,128)}, s32[128]{0:T(128)S(1)}, /*index=...) while((s32[]{:T(128)}, f32[128,3,3,64]{0,3,2,1:T(8,128)}, ...), condition=%wide.region_14.15_spmd.clone, body=%wide.region_13.14_spmd.clone.sunk | while | flops 152977408 | bytes 2845815 | solution.py:121
  370.4 90.7 %while.78 = (s32[]{:T(128)}, f32[128,3,3,64]{0,3,2,1:T(8,128)}, bf16[8,512,384]{2,1,0:T(8,128)(2,1)}, bf16[8,512,384]{1,2,0:T(8,128)(2,1)}, s32[8,512]{1,0:T(8,1...) while((s32[]{:T(128)}, f32[128,3,3,64]{0,3,2,1:T(8,128)}, ...), condition=%wide.region_18.19_spmd.clone, body=%wide.region_17.18_spmd.clone.sunk | while | flops 383205376 | bytes 17996008 | solution.py:223
  463.3 75.9 %reduce-scatter.49.cloned.1.call-done = bf16[128,384]{1,0:T(8,128)(2,1)} async-done(((bf16[4096,384]{1,0:T(8,128)(2,1)}), bf16[128,384]{1,0:T(8,128)(2,1)}) %reduce-scatter.49.cloned.1.call-update) | async-done | bytes 98320
  551.8 83.7 %while.79 = (s32[]{:T(128)}, f32[128,3,3,64]{0,3,2,1:T(8,128)}, bf16[8,512,384]{2,1,0:T(8,128)(2,1)}, bf16[8,512,384]{1,2,0:T(8,128)(2,1)}, s32[8,512]{1,0:T(8,1...) while((s32[]{:T(128)}, f32[128,3,3,64]{0,3,2,1:T(8,128)}, ...), condition=%wide.region_23.24_spmd.clone, body=%wide.region_22.23_spmd.clone.sunk | while | flops 383205376 | bytes 18585860 | solution.py:223
  658.6 56.9 %reduce-scatter.51.cloned.1.call-done = bf16[128,384]{1,0:T(8,128)(2,1)} async-done(((bf16[4096,384]{1,0:T(8,128)(2,1)}), bf16[128,384]{1,0:T(8,128)(2,1)}) %reduce-scatter.51.cloned.1.call-update) | async-done | bytes 98320
  719.8 27.7 %reduce-scatter.55.cloned.1.call-done = bf16[384,576]{1,0:T(8,128)(2,1)} async-done(((bf16[1536,576]{1,0:T(8,128)(2,1)}), bf16[384,576]{1,0:T(8,128)(2,1)}) %reduce-scatter.55.cloned.1.call-update) | async-done | bytes 442384
  749.5 28.7 %reduce-scatter.53.cloned.1.call-done = bf16[384,576]{1,0:T(8,128)(2,1)} async-done(((bf16[1536,576]{1,0:T(8,128)(2,1)}), bf16[384,576]{1,0:T(8,128)(2,1)}) %reduce-scatter.53.cloned.1.call-update) | async-done | bytes 442384
  780.2 21.9 %reduce-scatter.27.cloned.1.call-done = bf16[144,576]{1,0:T(8,128)(2,1)} async-done(((bf16[576,576]{1,0:T(8,128)(2,1)}), bf16[144,576]{1,0:T(8,128)(2,1)}) %reduce-scatter.27.cloned.1.call-update) | async-done | bytes 165904 | tf_op jit(solution)/shard_map/reduce_scatter | solution.py:340
  802.0 24.3 %reduce-scatter.39.cloned.1.call-done = bf16[144,576]{1,0:T(8,128)(2,1)} async-done(((bf16[576,576]{1,0:T(8,128)(2,1)}), bf16[144,576]{1,0:T(8,128)(2,1)}) %reduce-scatter.39.cloned.1.call-update) | async-done | bytes 165904 | tf_op jit(solution)/shard_map/reduce_scatter | solution.py:349
  826.3 30.8 %reduce-scatter.43.cloned.1.call-done = bf16[144,1536]{1,0:T(8,128)(2,1)} async-done(((bf16[576,1536]{1,0:T(8,128)(2,1)}), bf16[144,1536]{1,0:T(8,128)(2,1)}) %reduce-scatter.43.cloned.1.call-update) | async-done | bytes 442384 | tf_op jit(solution)/shard_map/reduce_scatter | solution.py:352
  857.1 29.8 %reduce-scatter.47.cloned.1.call-done = bf16[144,1536]{1,0:T(8,128)(2,1)} async-done(((bf16[576,1536]{1,0:T(8,128)(2,1)}), bf16[144,1536]{1,0:T(8,128)(2,1)}) %reduce-scatter.47.cloned.1.call-update) | async-done | bytes 442384 | tf_op jit(solution)/shard_map/reduce_scatter | solution.py:355
  886.9 23.8 %reduce-scatter.25.cloned.1.call-done = bf16[144,576]{1,0:T(8,128)(2,1)} async-done(((bf16[576,576]{1,0:T(8,128)(2,1)}), bf16[144,576]{1,0:T(8,128)(2,1)}) %reduce-scatter.25.cloned.1.call-update) | async-done | bytes 165904 | tf_op jit(solution)/shard_map/reduce_scatter | solution.py:340
  910.6 24.3 %reduce-scatter.37.cloned.1.call-done = bf16[144,576]{1,0:T(8,128)(2,1)} async-done(((bf16[576,576]{1,0:T(8,128)(2,1)}), bf16[144,576]{1,0:T(8,128)(2,1)}) %reduce-scatter.37.cloned.1.call-update) | async-done | bytes 165904 | tf_op jit(solution)/shard_map/reduce_scatter | solution.py:349
  934.9 30.9 %reduce-scatter.41.cloned.1.call-done = bf16[144,1536]{1,0:T(8,128)(2,1)} async-done(((bf16[576,1536]{1,0:T(8,128)(2,1)}), bf16[144,1536]{1,0:T(8,128)(2,1)}) %reduce-scatter.41.cloned.1.call-update) | async-done | bytes 442384 | tf_op jit(solution)/shard_map/reduce_scatter | solution.py:352
  965.8 29.2 %reduce-scatter.45.cloned.1.call-done = bf16[144,1536]{1,0:T(8,128)(2,1)} async-done(((bf16[576,1536]{1,0:T(8,128)(2,1)}), bf16[144,1536]{1,0:T(8,128)(2,1)}) %reduce-scatter.45.cloned.1.call-update) | async-done | bytes 442384 | tf_op jit(solution)/shard_map/reduce_scatter | solution.py:355
  1016.1 22.8 %reduce-scatter.35.cloned.1.call-done = bf16[144,192]{1,0:T(8,128)(2,1)} async-done(((bf16[576,192]{1,0:T(8,128)(2,1)}), bf16[144,192]{1,0:T(8,128)(2,1)}) %reduce-scatter.35.cloned.1.call-update) | async-done | bytes 55312 | tf_op jit(solution)/shard_map/reduce_scatter | solution.py:346
  1038.9 23.4 %reduce-scatter.29.cloned.1.call-done = bf16[144,192]{1,0:T(8,128)(2,1)} async-done(((bf16[576,192]{1,0:T(8,128)(2,1)}), bf16[144,192]{1,0:T(8,128)(2,1)}) %reduce-scatter.29.cloned.1.call-update) | async-done | bytes 55312 | tf_op jit(solution)/shard_map/reduce_scatter | solution.py:343
  1062.4 22.7 %reduce-scatter.33.cloned.1.call-done = bf16[144,192]{1,0:T(8,128)(2,1)} async-done(((bf16[576,192]{1,0:T(8,128)(2,1)}), bf16[144,192]{1,0:T(8,128)(2,1)}) %reduce-scatter.33.cloned.1.call-update) | async-done | bytes 55312 | tf_op jit(solution)/shard_map/reduce_scatter | solution.py:346
  1085.1 119.0 %all-reduce.25.cloned.1.call-done = (bf16[1,144,576]{2,1,0:T(8,128)(2,1)}, bf16[1,144,576]{2,1,0:T(8,128)(2,1)}, bf16[1,144,576]{2,1,0:T(8,128)(2,1)}, bf16[1,14...) async-done(((bf16[1,144,576]{2,1,0:T(8,128)(2,1)}, ...) | async-done | bytes 3317776 | tf_op jit(solution)/shard_map/psum | solution.py:369
  1212.3 99.2 %all-reduce.23.cloned.1.call-done = (bf16[1,144,192]{2,1,0:T(8,128)(2,1)}, bf16[1,144,192]{2,1,0:T(8,128)(2,1)}, bf16[1,144,192]{2,1,0:T(8,128)(2,1)}, bf16[1,14...) async-done(((bf16[1,144,192]{2,1,0:T(8,128)(2,1)}, ...) | async-done | bytes 222352 | tf_op jit(solution)/shard_map/psum | solution.py:370
  (994 shorter events, 566.1 us)
Async XLA Ops:
  50.2 128.6 %all-gather.31.cloned.1.call-start = ((), (), s32[]{:S(2)}) async-start(), calls=%async_computation.30 | async-start | bytes 2211840 | tf_op jit(solution)/shard_map/all_gather | solution.py:293
  51.3 129.6 %all-gather.33.cloned.1.call-start = ((), (), s32[]{:S(2)}) async-start(), calls=%async_computation.31 | async-start | bytes 2211840 | tf_op jit(solution)/shard_map/all_gather | solution.py:294
  52.3 143.5 %all-gather.35.cloned.1.call-start = ((), (), s32[]{:S(2)}) async-start(), calls=%async_computation.32 | async-start | bytes 2211840 | tf_op jit(solution)/shard_map/all_gather | solution.py:295
  53.5 180.2 %all-gather.41.cloned.1.call-start = ((), (), s32[]{:S(2)}) async-start(), calls=%async_computation.35 | async-start | bytes 2211840 | tf_op jit(solution)/shard_map/all_gather | solution.py:295
  54.1 228.9 %all-gather.29.cloned.1.call-start = ((), (), s32[]{:S(2)}) async-start(), calls=%async_computation.17 | async-start | bytes 3244032 | tf_op jit(solution)/shard_map/all_gather | solution.py:86
  199.6 156.4 %all-gather.39.cloned.1.call-start = ((), (), s32[]{:S(2)}) async-start(), calls=%async_computation.34 | async-start | bytes 2211840 | tf_op jit(solution)/shard_map/all_gather | solution.py:294
  200.3 158.6 %all-gather.37.cloned.1.call-start = ((), (), s32[]{:S(2)}) async-start(), calls=%async_computation.33 | async-start | bytes 2211840 | tf_op jit(solution)/shard_map/all_gather | solution.py:293
  201.1 338.1 %reduce-scatter.49.cloned.1.call-start = ((), (), s32[]{:S(2)}) async-start(), calls=%async_computation.36 | async-start | bytes 3244032
  461.2 254.3 %reduce-scatter.51.cloned.1.call-start = ((), (), s32[]{:S(2)}) async-start(), calls=%async_computation.37 | async-start | bytes 3244032
  639.5 138.6 %reduce-scatter.53.cloned.1.call-start = ((), (), s32[]{:S(2)}) async-start(), calls=%async_computation.38 | async-start | bytes 2457600
  642.6 159.5 %reduce-scatter.27.cloned.1.call-start = ((), (), s32[]{:S(2)}) async-start(), calls=%async_computation.19 | async-start | bytes 921600 | tf_op jit(solution)/shard_map/reduce_scatter | solution.py:340
  643.9 182.5 %reduce-scatter.39.cloned.1.call-start = ((), (), s32[]{:S(2)}) async-start(), calls=%async_computation.25 | async-start | bytes 921600 | tf_op jit(solution)/shard_map/reduce_scatter | solution.py:349
  645.2 211.9 %reduce-scatter.43.cloned.1.call-start = ((), (), s32[]{:S(2)}) async-start(), calls=%async_computation.27 | async-start | bytes 2211840 | tf_op jit(solution)/shard_map/reduce_scatter | solution.py:352
  647.1 239.7 %reduce-scatter.47.cloned.1.call-start = ((), (), s32[]{:S(2)}) async-start(), calls=%async_computation.29 | async-start | bytes 2211840 | tf_op jit(solution)/shard_map/reduce_scatter | solution.py:355
  649.0 261.6 %reduce-scatter.25.cloned.1.call-start = ((), (), s32[]{:S(2)}) async-start(), calls=%async_computation.18 | async-start | bytes 921600 | tf_op jit(solution)/shard_map/reduce_scatter | solution.py:340
  651.2 283.7 %reduce-scatter.37.cloned.1.call-start = ((), (), s32[]{:S(2)}) async-start(), calls=%async_computation.24 | async-start | bytes 921600 | tf_op jit(solution)/shard_map/reduce_scatter | solution.py:349
  652.6 313.2 %reduce-scatter.41.cloned.1.call-start = ((), (), s32[]{:S(2)}) async-start(), calls=%async_computation.26 | async-start | bytes 2211840 | tf_op jit(solution)/shard_map/reduce_scatter | solution.py:352
  654.5 340.5 %reduce-scatter.45.cloned.1.call-start = ((), (), s32[]{:S(2)}) async-start(), calls=%async_computation.28 | async-start | bytes 2211840 | tf_op jit(solution)/shard_map/reduce_scatter | solution.py:355
  656.4 359.7 %reduce-scatter.31.cloned.1.call-start = ((), (), s32[]{:S(2)}) async-start(), calls=%async_computation.21 | async-start | bytes 368640 | tf_op jit(solution)/shard_map/reduce_scatter | solution.py:343
  657.5 381.5 %reduce-scatter.35.cloned.1.call-start = ((), (), s32[]{:S(2)}) async-start(), calls=%async_computation.23 | async-start | bytes 368640 | tf_op jit(solution)/shard_map/reduce_scatter | solution.py:346
  658.6 403.8 %reduce-scatter.29.cloned.1.call-start = ((), (), s32[]{:S(2)}) async-start(), calls=%async_computation.20 | async-start | bytes 368640 | tf_op jit(solution)/shard_map/reduce_scatter | solution.py:343
  717.5 367.5 %reduce-scatter.33.cloned.1.call-start = ((), (), s32[]{:S(2)}) async-start(), calls=%async_computation.22 | async-start | bytes 368640 | tf_op jit(solution)/shard_map/reduce_scatter | solution.py:346
  719.8 484.4 %all-reduce.25.cloned.1.call-start = ((), (), s32[]{:S(2)}) async-start(), calls=%async_computation.41 | async-start | bytes 6782976 | tf_op jit(solution)/shard_map/psum | solution.py:369
  995.0 316.5 %all-reduce.23.cloned.1.call-start = ((), (), s32[]{:S(2)}) async-start(), calls=%async_computation.40 | async-start | bytes 598016 | tf_op jit(solution)/shard_map/psum | solution.py:370
  (176 other events, 3030.2 us)
Sparse Core Ops, SparseCore 0:
  50.3 56.0 all-gather.26
  108.6 27.1 all-gather.30
  138.0 28.0 all-gather.32
  167.7 28.1 all-gather.34
  198.0 35.7 all-gather.40
  235.8 47.1 all-gather.28
  285.2 27.1 all-gather.38
  314.0 28.0 all-gather.36
  461.3 77.8 reduce-scatter.48
  635.7 79.7 reduce-scatter.50
  717.9 29.5 reduce-scatter.54
  749.8 28.3 reduce-scatter.52
  781.1 20.8 reduce-scatter.26
  804.3 21.9 reduce-scatter.38
  829.2 27.8 reduce-scatter.42
  860.1 26.7 reduce-scatter.46
  889.7 20.8 reduce-scatter.24
  912.9 21.9 reduce-scatter.36
  937.9 27.8 reduce-scatter.40
  968.2 26.7 reduce-scatter.44
  1041.9 20.4 reduce-scatter.28
  1064.6 20.4 reduce-scatter.32
  1089.8 114.2 all-reduce.24
  1209.3 102.1 all-reduce.22
  (2 shorter events, 38.4 us)
where the time goes:
time: 1330 us; the launch traced here: 1320 us
  waiting for transfers between devices  765 us (58%)
  matrix products  242 us (18%)
  local copies, waits for them, and re-layouts  147 us (11%)
  blocking collectives  107 us (8%)
  other arithmetic  39.9 us (3%)
  between operations  18.6 us (1%)
    unnamed x30, waiting for transfers between devices  191 us
    psum x1, waiting for transfers between devices, body(): lax.psum(shard_grads[0].astype(jnp.bfloat16), 'ctx').astype(jnp.float32)  119 us
    psum x1, waiting for transfers between devices, body(): lax.psum(shard_grads[1].astype(jnp.bfloat16), 'ctx').astype(jnp.float32)  99.2 us
    reduce_scatter x2, waiting for transfers between devices, body(): lax.psum_scatter(grad_gate.astype(jnp.bfloat16), 'dp', scatter_dimension=...  61.6 us
    reduce_scatter x2, waiting for transfers between devices, body(): lax.psum_scatter(grad_up.astype(jnp.bfloat16), 'dp', scatter_dimension=0,...  59 us
    all_gather x2, waiting for transfers between devices, layer_forward(): all_kv = lax.all_gather(local_kv, 'ctx', axis=0, tiled=True)  49.9 us
    squeeze x48, local copies, waits for them, and re-layouts, layer_forward(): lax.scan(stats_step, (start_max, jnp.zeros_like(start_max)), (kv_stack, p...  49.6 us
    reduce_scatter x2, waiting for transfers between devices, body(): lax.psum_scatter(grad_out.astype(jnp.bfloat16), 'dp', scatter_dimension=0...  48.6 us
  transfers between devices with their start and end apart: 26, of which 22 were waited for; matrix products, arithmetic and copies ran while one was open for 16% of the time, Pallas kernels for 0%

commit v1 on v0

v1 whole, which is shorter than its diff:
```python
import functools

import jax
import jax.numpy as jnp
from jax import lax
from jax.experimental import pallas as pl
from jax.experimental.pallas import tpu as pltpu
from jax.sharding import PartitionSpec as P

HEADS = 9
KV = 3
HD = 64
LAYERS = 2
D = 576
FF = 1536
NX = 4
NZ = 4
NY = 4
NORM_EPS = 1e-05
ROPE_BASE = 100000.0
NEG = -1e30
BIG = 1e30
MESH = pl.DeviceIdType.MESH
ALL = slice(None)
F32 = jnp.float32
BF = jnp.bfloat16
VMEM_LIMIT = 60 * 1024 * 1024


def place():
    ctx = lax.axis_index("ctx")
    return lax.div(ctx, 8), lax.rem(lax.div(ctx, 2), 4), lax.rem(ctx, 2)


def ctx_of(x, z, c):
    return (x * NZ + z) * 2 + c


def turn(i, d):
    return lax.rem(i + (d + 4), 4)


def neighbour(axis, d):
    x, z, c = place()
    return ctx_of(turn(x, d), z, c) if axis == 0 else ctx_of(x, turn(z, d), c)


def other_core():
    x, z, c = place()
    return ctx_of(x, z, 1 - c)


def greet(dp_too):
    barrier = pltpu.get_barrier_semaphore()
    ids = [neighbour(0, 1), neighbour(0, -1), neighbour(1, 1), neighbour(1, -1), other_core()]
    for i in ids:
        pl.semaphore_signal(barrier, inc=1, device_id={"ctx": i}, device_id_type=MESH)
    count = len(ids)
    if dp_too:
        y = lax.axis_index("dp")
        for k in (1, 2, 3):
            pl.semaphore_signal(barrier, inc=1, device_id={"dp": turn(y, k)}, device_id_type=MESH)
        count += 3
    pl.semaphore_wait(barrier, count)


class Wire:
    def __init__(self, send, recv):
        self.send, self.recv, self.open = send, recv, []

    def desc(self, src, dst, k, dev):
        return pltpu.make_async_remote_copy(
            src_ref=src,
            dst_ref=dst,
            send_sem=self.send.at[k],
            recv_sem=self.recv.at[k],
            device_id=dev,
            device_id_type=MESH,
        )

    def go(self, src, dst, k, dev):
        copy = self.desc(src, dst, k, dev)
        copy.start()
        self.open.append(copy)

    def got(self, dst, k, dev):
        self.desc(dst, dst, k, dev).wait_recv()

    def close(self):
        for copy in self.open:
            copy.wait_send()
        self.open = []


def run_all(gens):
    gens = list(gens)
    while gens:
        left = []
        for g in gens:
            try:
                next(g)
                left.append(g)
            except StopIteration:
                pass
        gens = left


def gather_half(wire, base, h, view, core_too):
    x, z, c = place()
    axes = (0, 1) if h == 0 else (1, 0)
    pos = (x, z) if h == 0 else (z, x)
    oth = {"ctx": other_core()}
    for stage in (0, 1):
        axis, me = axes[stage], pos[stage]
        right, left = {"ctx": neighbour(axis, 1)}, {"ctx": neighbour(axis, -1)}
        b = base + 4 * stage

        def at(i, part):
            return view(i, pos[1], part, c) if stage == 0 else view(ALL, i, part, c)

        def share(i, k):
            if stage == 1 and core_too:
                wire.go(at(i, None), at(i, None), base + 8 + k, oth)

        wire.go(at(me, None), at(me, None), b, right)
        wire.go(at(me, None), at(me, None), b + 1, left)
        share(me, 0)
        yield
        wire.got(at(turn(me, -1), None), b, left)
        wire.go(at(turn(me, -1), 0), at(turn(me, -1), 0), b + 2, right)
        share(turn(me, -1), 1)
        yield
        wire.got(at(turn(me, 1), None), b + 1, right)
        wire.go(at(turn(me, 1), 1), at(turn(me, 1), 1), b + 3, left)
        share(turn(me, 1), 2)
        yield
        wire.got(at(turn(me, 2), 0), b + 2, left)
        wire.got(at(turn(me, 2), 1), b + 3, right)
        share(turn(me, 2), 3)
        yield
    if core_too:
        me = pos[1]
        for k, d in enumerate((0, -1, 1, 2)):
            wire.got(view(ALL, turn(me, d), None, 1 - c), base + 8 + k, oth)


def add_into(dst, *srcs):
    if len(dst.shape) > 2:

        def step(i, carry):
            add_into(dst.at[i], *[s.at[i] for s in srcs])
            return carry

        if len(dst.shape) == 3:
            for i in range(dst.shape[0]):
                step(i, 0)
        else:
            lax.fori_loop(0, dst.shape[0], step, 0)
        return
    total = dst[...].astype(F32)
    for s in srcs:
        total = total + s[...].astype(F32)
    dst[...] = total.astype(dst.dtype)


def scatter_half(wire, base, h, view, core_src, core_dst, slots):
    x, z, c = place()
    axes = (1, 0) if h == 0 else (0, 1)
    pos = (z, x) if h == 0 else (x, z)
    oth = {"ctx": other_core()}
    order = (2, 1, -1, 0)
    if core_src is not None:
        for k, d in enumerate(order):
            f = turn(pos[0], d)
            wire.go(core_src(f), core_dst(f), base + k, oth)
        yield

    def core_sum(k):
        f = turn(pos[0], order[k])
        wire.got(core_dst(f), base + k, oth)
        add_into(view(f, ALL, None), core_dst(f))

    for stage in (0, 1):
        axis, me = axes[stage], pos[stage]
        right, left = {"ctx": neighbour(axis, 1)}, {"ctx": neighbour(axis, -1)}
        b = base + 4 + 4 * stage
        one_a, one_b, two_a, two_b = slots[stage]

        def at(i, part):
            return view(i, ALL, part) if stage == 0 else view(pos[0], i, part)

        if stage == 0:
            core_sum(0)
        wire.go(at(turn(me, 2), 0), one_a, b, right)
        wire.go(at(turn(me, 2), 1), one_b, b + 1, left)
        yield
        if stage == 0:
            core_sum(1)
            core_sum(2)
        wire.got(one_a, b, left)
        add_into(at(turn(me, 1), 0), one_a)
        wire.go(at(turn(me, 1), None), two_a, b + 2, right)
        yield
        wire.got(one_b, b + 1, right)
        add_into(at(turn(me, -1), 1), one_b)
        wire.go(at(turn(me, -1), None), two_b, b + 3, left)
        yield
        if stage == 0:
            core_sum(3)
        wire.got(two_a, b + 2, left)
        wire.got(two_b, b + 3, right)
        add_into(at(me, None), two_a, two_b)
        yield


def lanes(shape):
    return lax.broadcasted_iota(jnp.int32, shape, len(shape) - 1)


def mm(a, b):
    return lax.dot_general(a, b, (((1,), (0,)), ((), ())), preferred_element_type=F32)


def mm_t(a, b):
    return lax.dot_general(a, b, (((1,), (1,)), ((), ())), preferred_element_type=F32)


def tmm(a, b):
    return lax.dot_general(a, b, (((0,), (0,)), ((), ())), preferred_element_type=F32)


def inv_rms(v):
    return lax.rsqrt(jnp.mean(v * v, axis=-1, keepdims=True) + NORM_EPS)


def norm_back(v, g, d):
    r = inv_rms(v)
    dv = r * g * d - v * (r * r * r * jnp.mean(g * d * v, axis=-1, keepdims=True))
    return dv, jnp.sum(d * v * r, axis=0, keepdims=True)


def rope(t, cos, ssin):
    first = lax.rem(lanes(t.shape), HD) < HD // 2
    turned = jnp.where(first, pltpu.roll(t, 96, 1), pltpu.roll(t, 32, 1))
    return t * cos + turned * ssin


def pair(t, half):
    lo, hi = t[:64], t[64:]
    first = lanes((64, 128)) < HD
    if half == 0:
        return jnp.where(first, lo, pltpu.roll(hi, HD, 1))
    return jnp.where(first, pltpu.roll(lo, HD, 1), hi)


def unpair(a, b):
    first = lanes((64, 128)) < HD
    lo = jnp.where(first, a, pltpu.roll(b, HD, 1))
    hi = jnp.where(first, pltpu.roll(a, HD, 1), b)
    return jnp.concatenate([lo, hi], axis=0)


def tile(v, i):
    return v[:, 128 * i : 128 * i + 128]


def doubled(p):
    first = lanes((192, 128)) < HD
    one = jnp.where(first, pltpu.roll(p, HD, 1), 0.0)
    zero = jnp.zeros((192, 128), F32)
    return jnp.concatenate(
        [jnp.concatenate([one, zero], axis=1), jnp.concatenate([zero, p], axis=1)], axis=0
    ).astype(BF)


def slot_row(scal, c, row_a, row_b):
    pick = jnp.full((1, 384), scal[2, c], F32) > 0.5
    own = jnp.full((1, 384), scal[3, c], F32)
    extra = jnp.where(lanes((1, 384)) >= 192, own, 0.0)
    return jnp.where(pick, row_a, row_b), extra


def w_mat(wv, kind, i):
    return wv[kind, i].reshape(D, 384)


def w_down(wv, i):
    return wv[3, :, i].reshape(D, 384)


def load_weights(w_any, layer, wv, sems):
    return [
        pltpu.make_async_copy(w_any.at[layer, k], wv.at[k], sems.at[k]) for k in range(4)
    ]


def chunk_of(buf, ci, i):
    return buf[ci // 2, pl.ds(2 * (ci % 2), 2), :, i].reshape(256, 128)


def diag_keys(k):
    first = lanes((64, 128)) < HD
    zero = jnp.zeros((64, 128), k.dtype)
    both = jnp.concatenate([jnp.where(first, k, zero), jnp.where(first, zero, k)], axis=0)
    return both


def diag_bias():
    shape = (128, 384)
    key = lax.rem(lax.broadcasted_iota(jnp.int32, shape, 0), 64)
    q = lanes(shape)
    visible = (q >= 192) & (key <= lax.rem(q, 64))
    return jnp.where(visible, 0.0, NEG)


def weights_kernel(win, gin, w_out, g_out, send, recv, loc):
    x, z, c = place()
    y = lax.axis_index("dp")
    greet(True)
    wire = Wire(send, recv)
    own = pltpu.make_async_copy(win.at[c, x, z], w_out.at[c, x, z, y], loc.at[0])
    own.start()
    gown = pltpu.make_async_copy(gin, g_out.at[y], loc.at[1])
    gown.start()
    for k in (1, 2, 3):
        dev = {"dp": turn(y, k)}
        wire.go(win.at[c, x, z], w_out.at[c, x, z, y], 24 + k, dev)
        wire.go(gin, g_out.at[y], 28 + k, dev)
    own.wait()
    gown.wait()
    for k in (1, 2, 3):
        dev = {"dp": turn(y, k)}
        wire.got(w_out.at[c, x, z, turn(y, -k)], 24 + k, dev)
        wire.got(g_out.at[turn(y, -k)], 28 + k, dev)

    rows = {None: pl.ds(0, 144), 0: pl.ds(0, 64), 1: pl.ds(64, 80)}

    def view_of(h):
        def view(first, second, part, core):
            xi, zi = (first, second) if h == 0 else (second, first)
            return w_out.at[core, xi, zi, pl.ds(2 * h, 2), rows[part]]

        return view

    run_all([gather_half(wire, 12 * h, h, view_of(h), True) for h in (0, 1)])
    wire.close()


def gather_weights(win, gin):
    any_spec = pl.BlockSpec(memory_space=pl.ANY)
    return pl.pallas_call(
        weights_kernel,
        out_shape=(
            jax.ShapeDtypeStruct((LAYERS, NX, NZ, NY, 144, 384), BF),
            jax.ShapeDtypeStruct((NY, 16, 256), BF),
        ),
        in_specs=[any_spec, any_spec],
        out_specs=(any_spec, any_spec),
        scratch_shapes=[
            pltpu.SemaphoreType.DMA((32,)),
            pltpu.SemaphoreType.DMA((32,)),
            pltpu.SemaphoreType.DMA((2,)),
        ],
        compiler_params=pltpu.CompilerParams(
            collective_id=0, has_side_effects=True, vmem_limit_bytes=VMEM_LIMIT
        ),
        name="gather_weights",
    )(win, gin)


def forward_kernel(
    layer, h_ref, w_any, gains, cos_ref, sin_ref, mask_ref, ind_ref, scal,
    next_ref, mid_ref, attn_ref, qt_ref, kv, lse_ref, op_ref,
    wv, s_scr, sd_scr, acc_scr, wide, send, recv, loc,
):
    x, z, c = place()
    loads = load_weights(w_any, layer, wv, loc)
    for k in (2, 0, 1, 3):
        loads[k].start()
    greet(False)
    h = h_ref[...]
    n1 = (h * inv_rms(h) * gains[0:1]).astype(BF)
    loads[2].wait()
    qkv = [mm(n1, w_mat(wv, 2, i)) for i in range(3)]
    tiles = [tile(qkv[i // 3], i % 3) for i in range(8)]
    cos, ssin = cos_ref[...], sin_ref[...]
    tiles[:6] = [rope(t, cos, ssin) for t in tiles[:6]]
    k_pairs = [pair(tiles[4], 1), pair(tiles[5], 0), pair(tiles[5], 1)]
    v_pairs = [pair(tiles[6], 0), pair(tiles[6], 1), pair(tiles[7], 0)]
    for i, p in enumerate(k_pairs + v_pairs):
        kv[x, z, c, i] = p.astype(BF)

    wire = Wire(send, recv)
    rows = {None: pl.ds(0, 64), 0: pl.ds(0, 32), 1: pl.ds(32, 32)}

    def view_of(hf):
        def view(first, second, part, core):
            xi, zi = (first, second) if hf == 0 else (second, first)
            return kv.at[xi, zi, core, pl.ds(3 * hf, 3), rows[part]]

        return view

    gens = [gather_half(wire, 12 * hf, hf, view_of(hf), True) for hf in (0, 1)]
    for g in gens:
        next(g)
    for k in range(KV):
        qp = jnp.concatenate(
            [pair(tiles[(3 * k + g) // 2], (3 * k + g) % 2) for g in range(3)], axis=0
        )
        qt_ref[k] = doubled(qp * 0.125)
    run_all(gens)
    wire.close()

    lane = lanes((1, 384))
    in_one = lane < 192
    bias = diag_bias()
    zero128 = jnp.zeros((128, 128), BF)
    own = [kv[x, z, c, i] for i in range(6)]
    runs = []
    for k in range(KV):
        sd = mm_t(jnp.concatenate([zero128, diag_keys(own[k])], axis=1), qt_ref[k]) + bias
        sd_scr[k] = sd
        lo = jnp.max(sd[:64].reshape(8, 8, 384), axis=0)
        hi = jnp.max(sd[64:].reshape(8, 8, 384), axis=0)
        runs += [jnp.full((8, 384), NEG, F32), lo, hi]

    def scores(ci, carry):
        carry = list(carry)
        m = mask_ref[ci]
        for k in range(KV):
            keys = chunk_of(kv, ci, k)
            s = mm_t(jnp.concatenate([keys, keys * m], axis=1), qt_ref[k])
            s_scr[k, ci] = s
            for i in range(4):
                top = jnp.max(s[64 * i : 64 * i + 64].reshape(8, 8, 384), axis=0)
                slot = 4 * ci + i
                carry[3 * k] = jnp.maximum(carry[3 * k], top)
                carry[3 * k + 1] = jnp.maximum(carry[3 * k + 1], top + scal[0, slot])
                carry[3 * k + 2] = jnp.maximum(carry[3 * k + 2], top + scal[1, slot])
        return tuple(carry)

    runs = lax.fori_loop(0, 8, scores, tuple(runs))
    row_a, row_b = [], []
    for k in range(KV):
        one, lo, hi = [jnp.max(r, axis=0, keepdims=True) for r in runs[3 * k : 3 * k + 3]]
        top = jnp.where(in_one, one, hi)
        top = jnp.maximum(top, pltpu.roll(top, 192, 1))
        row_a.append(jnp.where(in_one, top, lo))
        row_b.append(top)

    dlane = lanes((128, 128))
    drow = lax.broadcasted_iota(jnp.int32, (128, 128), 0)
    dind = jnp.where(
        ((dlane == 65) & (drow < 64)) | ((dlane == 66) & (drow >= 64)), 1.0, 0.0
    ).astype(BF)
    for k in range(KV):
        sd = sd_scr[k]
        p = jnp.concatenate([jnp.exp(sd[:64] - row_a[k]), jnp.exp(sd[64:] - row_b[k])], axis=0)
        vals = jnp.concatenate([dind, diag_keys(own[3 + k])], axis=1)
        acc_scr[k] = tmm(vals, p.astype(BF))

    def values(ci, carry):
        m, ind = mask_ref[ci], ind_ref[ci]
        first = lanes((256, 128)) < HD
        for k in range(KV):
            s = s_scr[k, ci]
            parts = []
            for i in range(4):
                base, extra = slot_row(scal, 4 * ci + i, row_a[k], row_b[k])
                parts.append(jnp.exp(s[64 * i : 64 * i + 64] - (base + extra)))
            p = jnp.concatenate(parts, axis=0).astype(BF)
            v = chunk_of(kv, ci, 3 + k)
            vals = jnp.concatenate([jnp.where(first, v, ind), v * m], axis=1)
            acc_scr[k] += tmm(vals, p)
        return carry

    lax.fori_loop(0, 8, values, 0)

    pairs = []
    for k in range(KV):
        acc = acc_scr[k]
        rolled = pltpu.roll(acc, 192, 1)
        hi = acc[0:64] + rolled[192:256]
        lo = rolled[128:192]
        tot_hi = acc[64:65] + rolled[66:67]
        tot_lo = rolled[65:66]
        lse_hi = row_b[k] + jnp.log(jnp.where(in_one, tot_hi, 1.0))
        lse_hi = jnp.where(in_one, lse_hi, pltpu.roll(lse_hi, 192, 1))
        lse_lo = pltpu.roll(row_a[k], 192, 1) + jnp.log(jnp.where(in_one, tot_lo, 1.0))
        lse_ref[k, 0:1] = jnp.where(in_one, lse_hi, pltpu.roll(lse_lo, 192, 1))
        lse_ref[k, 1:2] = lse_hi
        lse_ref[k, 2:8] = jnp.zeros((6, 384), F32)
        out_t = jnp.concatenate(
            [lo / jnp.where(in_one, tot_lo, 1.0), hi / jnp.where(in_one, tot_hi, 1.0)], axis=0
        )
        p = jnp.transpose(out_t)[:192]
        op_ref[k] = p
        pairs += [p[64 * g : 64 * g + 64] for g in range(3)]
    pairs.append(jnp.zeros((64, 128), F32))
    attn = jnp.concatenate(
        [unpair(pairs[2 * t], pairs[2 * t + 1]) for t in range(5)], axis=1
    ).astype(BF)
    attn_ref[...] = attn
    a = attn[:, :D]
    proj = jnp.concatenate([mm(a, w_mat(wv, 2, 2)), mm(a, w_mat(wv, 2, 3))], axis=1)
    mid = h + pltpu.roll(proj, D, 1)[:, :D]
    mid_ref[...] = mid
    n2 = (mid * inv_rms(mid) * gains[1:2]).astype(BF)
    for k in (0, 1, 3):
        loads[k].wait()
    for i in range(4):
        gate = mm(n2, w_mat(wv, 0, i))
        up = mm(n2, w_mat(wv, 1, i))
        inner = (gate * jax.nn.sigmoid(gate) * up).astype(BF)
        mid = mid + mm_t(inner, w_down(wv, i))
    next_ref[...] = mid


def forward_layer(layer, h, w, gains, cos, ssin, mask, ind, scal):
    vm = pl.BlockSpec(memory_space=pltpu.VMEM)
    return pl.pallas_call(
        functools.partial(forward_kernel, layer),
        out_shape=(
            jax.ShapeDtypeStruct((128, D), F32),
            jax.ShapeDtypeStruct((128, D), F32),
            jax.ShapeDtypeStruct((128, 640), BF),
            jax.ShapeDtypeStruct((KV, 384, 256), BF),
            jax.ShapeDtypeStruct((NX, NZ, 2, 6, 64, 128), BF),
            jax.ShapeDtypeStruct((KV, 8, 384), F32),
            jax.ShapeDtypeStruct((KV, 192, 128), F32),
        ),
        in_specs=[vm, pl.BlockSpec(memory_space=pl.ANY), vm, vm, vm, vm, vm,
                  pl.BlockSpec(memory_space=pltpu.SMEM)],
        out_specs=(vm,) * 7,
        scratch_shapes=[
            pltpu.VMEM((4, 4, 4, 144, 384), BF),
            pltpu.VMEM((KV, 8, 256, 384), F32),
            pltpu.VMEM((KV, 128, 384), F32),
            pltpu.VMEM((KV, 256, 384), F32),
            pltpu.VMEM((128, 640), F32),
            pltpu.SemaphoreType.DMA((24,)),
            pltpu.SemaphoreType.DMA((24,)),
            pltpu.SemaphoreType.DMA((4,)),
        ],
        compiler_params=pltpu.CompilerParams(
            collective_id=1 + layer, has_side_effects=True, vmem_limit_bytes=VMEM_LIMIT
        ),
        name="forward_layer",
    )(h, w, gains, cos, ssin, mask, ind, scal)


def transposed(v, wide):
    wide[:, :D] = v.astype(F32)
    return jnp.transpose(wide[...])[:D].astype(BF)


def backward_kernel(
    layer, g_ref, h_ref, mid_ref, attn_ref, qt_ref, kv, lse_ref, op_ref, w_any, gains,
    cos_ref, sin_ref, mask_ref, scal,
    dh_ref, gw, gg_ref,
    wv, dot_scr, dq_scr, pbuf, rcore, one_a1, one_b1, two_a1, two_b1, one_a2, one_b2, two_a2,
    two_b2, wide, send, recv, loc,
):
    x, z, c = place()
    loads = load_weights(w_any, layer, wv, loc)
    for k in (0, 1, 3, 2):
        loads[k].start()
    greet(False)
    wide[...] = jnp.zeros((128, 640), F32)
    g = g_ref[...]
    mid = mid_ref[...]
    gain2 = gains[1:2]
    n2 = (mid * inv_rms(mid) * gain2).astype(BF)
    n2_t = transposed(n2, wide)
    branch = g.astype(BF)
    branch_t = transposed(branch, wide)
    d_n2 = jnp.zeros((128, D), F32)
    for k in (0, 1, 3):
        loads[k].wait()
    for i in range(4):
        gate_w, up_w, down_w = w_mat(wv, 0, i), w_mat(wv, 1, i), w_down(wv, i)
        gate = mm(n2, gate_w)
        up = mm(n2, up_w)
        sig = jax.nn.sigmoid(gate)
        act = gate * sig
        inner = (act * up).astype(BF)
        d_inner = mm(branch, down_w)
        d_gate = (d_inner * up * (sig + act * (1.0 - sig))).astype(BF)
        d_up = (d_inner * act).astype(BF)
        gw[0, i] = mm(n2_t, d_gate).astype(BF).reshape(4, 144, 384)
        gw[1, i] = mm(n2_t, d_up).astype(BF).reshape(4, 144, 384)
        gw[3, :, i] = mm(branch_t, inner).astype(BF).reshape(4, 144, 384)
        d_n2 = d_n2 + mm_t(d_gate, gate_w) + mm_t(d_up, up_w)
    d_hn, gg2 = norm_back(mid, gain2, d_n2)
    d_mid = g + d_hn
    gg_ref[1:2] = gg2
    gg_ref[2:8] = jnp.zeros((6, D), F32)
    loads[2].wait()
    wide[:, :D] = d_mid
    dm = jnp.concatenate([wide[...], jnp.zeros((128, 128), F32)], axis=1)
    dm = pltpu.roll(dm, 192, 1).astype(BF)
    d_attn = mm_t(dm[:, :384], w_mat(wv, 2, 2)) + mm_t(dm[:, 384:], w_mat(wv, 2, 3))
    wide[:, :D] = d_attn
    attn_t = jnp.transpose(attn_ref[...].astype(F32))[:D].astype(BF)
    g_out = mm(attn_t, dm)
    gw[2, 3] = g_out[:, 384:].astype(BF).reshape(4, 144, 384)
    gw[2, 2] = g_out[:, :384].astype(BF).reshape(4, 144, 384)
    da = wide[...].astype(BF).astype(F32)
    da_tiles = [tile(da, i) for i in range(5)]

    in_one = lanes((1, 384)) < 192
    pick_lo = jnp.where(
        lanes((16, 128)) < HD,
        jnp.where(lax.broadcasted_iota(jnp.int32, (16, 128), 0) == 0, 1.0, 0.0),
        jnp.where(lax.broadcasted_iota(jnp.int32, (16, 128), 0) == 1, 1.0, 0.0),
    ).astype(BF)
    delta_a, delta_b = [], []
    for k in range(KV):
        dp = jnp.concatenate(
            [pair(da_tiles[(3 * k + q) // 2], (3 * k + q) % 2) for q in range(3)], axis=0
        )
        dot_scr[k] = doubled(dp)
        prod = dp * op_ref[k]
        prod = jnp.concatenate([prod, prod], axis=0)
        coarse = prod.astype(BF)
        fine = (prod - coarse.astype(F32)).astype(BF)
        rows = mm_t(pick_lo, coarse) + mm_t(pick_lo, fine)
        lo, hi = rows[0:1], rows[1:2]
        delta_a.append(jnp.where(in_one, hi, lo))
        delta_b.append(hi)

    def back(k, keys2, vals2, subs, deltas, bias):
        s = mm_t(keys2, qt_ref[k])
        if bias is not None:
            s = s + bias
        dp = mm_t(vals2, dot_scr[k])
        probs, d_s = [], []
        for i, (sub, delta) in enumerate(zip(subs, deltas)):
            p = jnp.exp(s[64 * i : 64 * i + 64] - sub)
            probs.append(p.astype(BF))
            d_s.append((p * (dp[64 * i : 64 * i + 64] - delta)).astype(BF))
        probs = jnp.concatenate(probs, axis=0)
        d_s = jnp.concatenate(d_s, axis=0)
        return mm(d_s, qt_ref[k]), mm(probs, dot_scr[k]), tmm(keys2, d_s)

    def chunk(ci, carry):
        m = mask_ref[ci]
        mf = m.astype(F32)
        for k in range(KV):
            keys, vals = chunk_of(kv, ci, k), chunk_of(kv, ci, KV + k)
            subs, deltas = [], []
            for i in range(4):
                base, extra = slot_row(scal, 4 * ci + i, lse_ref[k, 0:1], lse_ref[k, 1:2])
                subs.append(base + extra)
                deltas.append(slot_row(scal, 4 * ci + i, delta_a[k], delta_b[k])[0])
            dk, dv, dq = back(
                k,
                jnp.concatenate([keys, keys * m], axis=1),
                jnp.concatenate([vals, vals * m], axis=1),
                subs,
                deltas,
                None,
            )
            first = lanes((256, 128)) < HD
            for j, d in ((k, dk), (KV + k, dv)):
                both = jnp.where(first, d[:, :128], 0.0) + mf * d[:, 128:]
                pbuf[ci // 2, pl.ds(2 * (ci % 2), 2), :, j] = both.astype(BF).reshape(2, 2, 64, 128)
            dq_scr[k] += dq
        return carry

    bias = diag_bias()
    zero128 = jnp.zeros((128, 128), BF)
    own_grads = []
    first = lanes((64, 128)) < HD
    for k in range(KV):
        dk, dv, dq = back(
            k,
            jnp.concatenate([zero128, diag_keys(kv[x, z, c, k])], axis=1),
            jnp.concatenate([zero128, diag_keys(kv[x, z, c, KV + k])], axis=1),
            [lse_ref[k, 0:1], lse_ref[k, 1:2]],
            [delta_a[k], delta_b[k]],
            bias,
        )
        own_grads.append([jnp.where(first, d[:64, 128:], d[64:, 128:]) for d in (dk, dv)])
        dq_scr[k] = dq
    lax.fori_loop(0, 8, chunk, 0)
    for k in range(KV):
        for j in (0, 1):
            part = pbuf.at[x, z, c, KV * j + k]
            part[...] = (part[...].astype(F32) + own_grads[k][j]).astype(BF)

    wire = Wire(send, recv)
    rws = {None: pl.ds(0, 64), 0: pl.ds(0, 32), 1: pl.ds(32, 32)}

    def half_of(hf):
        def xz(f, s):
            return (s, f) if hf == 0 else (f, s)

        heads = pl.ds(3 * hf, 3)

        def view(f, s, part):
            xi, zi = xz(f, s)
            return pbuf.at[xi, zi, c, heads, rws[part]]

        def core_src(f):
            xi, zi = xz(f, ALL)
            return pbuf.at[xi, zi, 1 - c, heads]

        def core_dst(f):
            xi, zi = xz(f, ALL)
            return rcore.at[xi, zi, heads]

        slots = (
            (one_a1.at[hf], one_b1.at[hf], two_a1.at[hf], two_b1.at[hf]),
            (one_a2.at[hf], one_b2.at[hf], two_a2.at[hf], two_b2.at[hf]),
        )
        return scatter_half(wire, 12 * hf, hf, view, core_src, core_dst, slots)

    gens = [half_of(hf) for hf in (0, 1)]
    for gen in gens:
        next(gen)

    h = h_ref[...]
    gain1 = gains[0:1]
    n1 = (h * inv_rms(h) * gain1).astype(BF)
    n1_t = transposed(n1, wide)
    cos, ssin = cos_ref[...], -sin_ref[...]
    pairs = []
    for k in range(KV):
        dq = dq_scr[k]
        rolled = pltpu.roll(dq, 192, 1)
        out_t = jnp.concatenate([rolled[128:192], dq[0:64] + rolled[192:256]], axis=0)
        p = jnp.transpose(out_t)[:192]
        pairs += [p[64 * q : 64 * q + 64] for q in range(3)]
    run_all(gens)
    wire.close()
    done = [pbuf[x, z, c, i].astype(F32) for i in range(6)]
    pairs += done
    pairs.append(jnp.zeros((64, 128), F32))
    first = lanes((128, 128)) < HD
    tiles = []
    for t in range(8):
        v = unpair(pairs[2 * t], pairs[2 * t + 1])
        if t < 6:
            v = rope(v, cos, ssin)
            if t < 4:
                v = v * 0.125
            elif t == 4:
                v = jnp.where(first, v * 0.125, v)
        tiles.append(v.astype(BF))
    tiles.append(jnp.zeros((128, 128), BF))
    d_n1 = jnp.zeros((128, D), F32)
    for i in range(3):
        d = jnp.concatenate(tiles[3 * i : 3 * i + 3], axis=1)
        gr = mm(n1_t, d)
        if i == 2:
            gr = gr + gw[2, 2].reshape(D, 384).astype(F32)
        gw[2, i] = gr.astype(BF).reshape(4, 144, 384)
        d_n1 = d_n1 + mm_t(d, w_mat(wv, 2, i))
    d_h, gg1 = norm_back(h, gain1, d_n1)
    gg_ref[0:1] = gg1
    dh_ref[...] = d_mid + d_h


def backward_layer(layer, g, saved, w, gains, cos, ssin, mask, scal):
    vm = pl.BlockSpec(memory_space=pltpu.VMEM)
    return pl.pallas_call(
        functools.partial(backward_kernel, layer),
        out_shape=(
            jax.ShapeDtypeStruct((128, D), F32),
            jax.ShapeDtypeStruct((4, 4, 4, 144, 384), BF),
            jax.ShapeDtypeStruct((8, D), F32),
        ),
        in_specs=[vm] * 8 + [pl.BlockSpec(memory_space=pl.ANY)] + [vm] * 4
        + [pl.BlockSpec(memory_space=pltpu.SMEM)],
        out_specs=(vm,) * 3,
        scratch_shapes=[
            pltpu.VMEM((4, 4, 4, 144, 384), BF),
            pltpu.VMEM((KV, 384, 256), BF),
            pltpu.VMEM((KV, 256, 384), F32),
            pltpu.VMEM((NX, NZ, 2, 6, 64, 128), BF),
            pltpu.VMEM((NX, NZ, 6, 64, 128), BF),
            pltpu.VMEM((2, 4, 3, 32, 128), BF),
            pltpu.VMEM((2, 4, 3, 32, 128), BF),
            pltpu.VMEM((2, 4, 3, 64, 128), BF),
            pltpu.VMEM((2, 4, 3, 64, 128), BF),
            pltpu.VMEM((2, 3, 32, 128), BF),
            pltpu.VMEM((2, 3, 32, 128), BF),
            pltpu.VMEM((2, 3, 64, 128), BF),
            pltpu.VMEM((2, 3, 64, 128), BF),
            pltpu.VMEM((128, 640), F32),
            pltpu.SemaphoreType.DMA((24,)),
            pltpu.SemaphoreType.DMA((24,)),
            pltpu.SemaphoreType.DMA((4,)),
        ],
        compiler_params=pltpu.CompilerParams(
            collective_id=3 + layer, has_side_effects=True, vmem_limit_bytes=VMEM_LIMIT
        ),
        name="backward_layer",
    )(g, *saved, w, gains, cos, ssin, mask, scal)


def reduce_kernel(
    g0, g1, out, part_sum, rcore, one_a1, one_b1, two_a1, two_b1, one_a2, one_b2, two_a2, two_b2,
    from_y, send, recv, loc,
):
    x, z, c = place()
    y = lax.axis_index("dp")
    greet(True)
    wire = Wire(send, recv)
    a_rows, b_rows = pl.ds(0, 64), pl.ds(64, 80)
    rws = {None: pl.ds(0, 144), 0: a_rows, 1: b_rows}
    load = pltpu.make_async_copy(g0, part_sum, loc.at[0])
    for core, keep in ((0, g0), (1, g1)):

        @pl.when(c == core)
        def _():
            pltpu.make_async_copy(keep, part_sum, loc.at[0]).start()

    load.wait()

    def half_of(hf):
        def xz(f, s):
            return (s, f) if hf == 0 else (f, s)

        ys = pl.ds(2 * hf, 2)

        def view(f, s, part):
            xi, zi = xz(f, s)
            return part_sum.at[xi, zi, ys, rws[part]]

        def core_dst(f):
            xi, zi = xz(f, ALL)
            return rcore.at[xi, zi, ys]

        slots = (
            (one_a1.at[hf], one_b1.at[hf], two_a1.at[hf], two_b1.at[hf]),
            (one_a2.at[hf], one_b2.at[hf], two_a2.at[hf], two_b2.at[hf]),
        )

        def start_core(src):
            f0 = z if hf == 0 else x
            for k, d in enumerate((2, 1, -1, 0)):
                f = turn(f0, d)
                xi, zi = xz(f, ALL)
                wire.desc(
                    src.at[xi, zi, ys], core_dst(f), 12 * hf + k, {"ctx": other_core()}
                ).start()

        return view, core_dst, slots, start_core

    halves = [half_of(hf) for hf in (0, 1)]
    for core, give in ((0, g1), (1, g0)):

        @pl.when(c == core)
        def _():
            for item in halves:
                item[3](give)

    gens = []
    for hf, (view, core_dst, slots, start_core) in enumerate(halves):
        gens.append(scatter_half(wire, 12 * hf, hf, view, None, core_dst, slots))
    run_all(gens)
    mine = part_sum.at[x, z]
    for k in (1, 2, 3):
        wire.go(mine.at[turn(y, k)], from_y.at[k - 1], 23 + k, {"dp": turn(y, k)})
    for k in (1, 2, 3):
        wire.got(from_y.at[k - 1], 23 + k, {"dp": turn(y, -k)})
    total = part_sum[x, z, y].astype(F32)
    for k in range(3):
        total = total + from_y[k].astype(F32)
    out[c, x, z] = total.astype(BF)
    parts = (
        {None: pl.ds(0, 64), 0: pl.ds(0, 32), 1: pl.ds(32, 32)},
        {None: pl.ds(64, 80), 0: pl.ds(64, 32), 1: pl.ds(96, 48)},
    )

    def view_of(h):
        def view(first, second, part, core):
            xi, zi = (first, second) if h == 0 else (second, first)
            return out.at[core, xi, zi, parts[h][part]]

        return view

    run_all([gather_half(wire, 27 + 12 * h, h, view_of(h), True) for h in (0, 1)])
    wire.close()
    for hf in (0, 1):
        for k in range(4):
            f = turn(z if hf == 0 else x, (2, 1, -1, 0)[k])
            dst = halves[hf][1](f)
            wire.desc(dst, dst, 12 * hf + k, {"ctx": other_core()}).wait_send()


def reduce_grads(g0, g1):
    any_spec = pl.BlockSpec(memory_space=pl.ANY)
    return pl.pallas_call(
        reduce_kernel,
        out_shape=jax.ShapeDtypeStruct((LAYERS, NX, NZ, 144, 384), BF),
        in_specs=[any_spec, any_spec],
        out_specs=pl.BlockSpec(memory_space=pltpu.VMEM),
        scratch_shapes=[
            pltpu.VMEM((NX, NZ, NY, 144, 384), BF),
            pltpu.VMEM((NX, NZ, NY, 144, 384), BF),
            pltpu.VMEM((2, 4, 2, 64, 384), BF),
            pltpu.VMEM((2, 4, 2, 80, 384), BF),
            pltpu.VMEM((2, 4, 2, 144, 384), BF),
            pltpu.VMEM((2, 4, 2, 144, 384), BF),
            pltpu.VMEM((2, 2, 64, 384), BF),
            pltpu.VMEM((2, 2, 80, 384), BF),
            pltpu.VMEM((2, 2, 144, 384), BF),
            pltpu.VMEM((2, 2, 144, 384), BF),
            pltpu.VMEM((3, 144, 384), BF),
            pltpu.SemaphoreType.DMA((51,)),
            pltpu.SemaphoreType.DMA((51,)),
            pltpu.SemaphoreType.DMA((1,)),
        ],
        compiler_params=pltpu.CompilerParams(
            collective_id=5, has_side_effects=True, vmem_limit_bytes=VMEM_LIMIT
        ),
        name="reduce_grads",
    )(g0, g1)


def pack_weights(wq, wk, wv, wo, wg, wu, wd):
    def blocks(w):
        return w.reshape(LAYERS, 144, 4, 384).transpose(0, 2, 1, 3)

    attn = jnp.concatenate([wq, wk, wv, wo], axis=2)
    down = wd.transpose(0, 2, 1).reshape(LAYERS, 4, 144, 384)
    return jnp.stack([blocks(wg), blocks(wu), blocks(attn), down], axis=1)


def unpack_grads(r):
    r = r.astype(F32)

    def cols(v):
        return v.transpose(0, 2, 1, 3).reshape(LAYERS, 144, 1536)

    attn = cols(r[:, 2])
    down = r[:, 3].reshape(LAYERS, D, 384).transpose(0, 2, 1)
    return (
        attn[:, :, :576], attn[:, :, 576:768], attn[:, :, 768:960], attn[:, :, 960:],
        cols(r[:, 0]), cols(r[:, 1]), down,
    )


def body(
    tokens, out_grad, w_query, w_key, w_value, w_out, w_gate, w_up, w_down_, attn_gain, ffn_gain,
    block_pairs,
):
    me = lax.axis_index("ctx")
    y = lax.axis_index("dp")
    mine = block_pairs[me]
    offs = jnp.arange(64, dtype=jnp.int32)
    pos = jnp.concatenate([mine * 64 + offs, (63 - mine) * 64 + offs])
    freq = ROPE_BASE ** (-2.0 * jnp.arange(HD // 2, dtype=F32) / HD)
    ang = pos.astype(F32)[:, None] * freq[None, :]
    cos = jnp.cos(ang)
    sin = jnp.sin(ang)
    cos = jnp.concatenate([cos] * 4, axis=1)
    ssin = jnp.concatenate([-sin, sin, -sin, sin], axis=1)
    is_lo = block_pairs < mine
    is_hi = block_pairs > mine
    scal = jnp.stack([
        jnp.where(is_lo, 0.0, NEG), jnp.where(is_hi, 0.0, NEG),
        jnp.where(is_lo, 1.0, 0.0), jnp.where(is_lo | is_hi, 0.0, BIG),
    ]).astype(F32)
    lane = jnp.arange(128)[None, :]
    lo_col = jnp.repeat(is_lo, 64)[:, None]
    hi_col = jnp.repeat(is_hi, 64)[:, None]
    mask = jnp.where(lane < 64, lo_col, hi_col).astype(BF).reshape(8, 256, 128)
    ind = ((lane == 64) | ((lane == 65) & lo_col) | ((lane == 66) & hi_col)).astype(BF)
    ind = ind.reshape(8, 256, 128)

    win = pack_weights(w_query, w_key, w_value, w_out, w_gate, w_up, w_down_)
    gin = jnp.zeros((16, 256), BF)
    gin = gin.at[0:2, :144].set(attn_gain).at[2:4, :144].set(ffn_gain)
    w, gall = gather_weights(win, gin)
    gall = gall[:, :4, :144].transpose(1, 0, 2).reshape(4, D).astype(F32)
    gains = [jnp.stack([gall[l], gall[2 + l]] + [gall[l]] * 6) for l in range(LAYERS)]

    h = tokens.astype(F32)
    states = []
    for l in range(LAYERS):
        nxt, mid, attn, qt, kv, lse, op = forward_layer(
            l, h, w, gains[l], cos, ssin, mask, ind, scal
        )
        states.append((h, mid, attn, qt, kv, lse, op))
        h = nxt
    result = h.astype(BF)
    g = out_grad.astype(F32)
    gws, ggs = [None] * 2, [None] * 2
    for l in (1, 0):
        g, gws[l], gg = backward_layer(l, g, states[l], w, gains[l], cos, ssin, mask, scal)
        ggs[l] = lax.psum(gg[:2], ("dp", "ctx"))
    grads = unpack_grads(reduce_grads(gws[0], gws[1]))
    gg = jnp.stack(ggs, axis=1)
    gg = lax.dynamic_slice(gg, (0, 0, y * 144), (2, LAYERS, 144))
    return (result, g) + grads + (gg[0], gg[1])


def solution(mesh):
    row = P(("dp", "ctx"), None)
    mat = P(None, "dp", None)
    vec = P(None, "dp")
    return jax.shard_map(
        body,
        mesh=mesh,
        in_specs=(row, row) + (mat,) * 7 + (vec, vec, P()),
        out_specs=(row, row) + (mat,) * 7 + (vec, vec),
        check_vma=False,
    )
```

time: 1330 us -> 417 us (0.31)
  waiting for transfers between devices: 765 us -> 0 us
  Pallas kernels: 0 us -> 314 us
  matrix products: 242 us -> 0 us
  local copies, waits for them, and re-layouts: 147 us -> 24.1 us
  blocking collectives: 107 us -> 64.2 us
  other arithmetic: 39.9 us -> 12.3 us
  between operations: 18.6 us -> 2.2 us
    pallas_call x0 -> x6, Pallas kernels: none -> 314 us  [the longest x2 94.5 us: backward_layer(): pl.pallas_call(functools.partial(backward_kernel, layer), out_shape=(jax....]
    reduce_scatter x12 -> x0, waiting for transfers between devices: 290 us -> none  [the longest x2 61.6 us: body(): lax.psum_scatter(grad_gate.astype(jnp.bfloat16), 'dp', scatter_dimension=...]
    dot_general x154 -> x0, matrix products: 242 us -> none  [the longest x32 47.1 us: masked_scores(): jnp.einsum('tkgd,skd->kgts', queries, key_block, preferred_element_type=j...]
    psum x2 -> x0, waiting for transfers between devices: 218 us -> none  [the longest x1 119 us: body(): lax.psum(shard_grads[0].astype(jnp.bfloat16), 'ctx').astype(jnp.float32)]
    unnamed x30 -> x0, waiting for transfers between devices: 191 us -> none
    all_gather x8 -> x0, blocking collectives: 92 us -> none  [the longest x2 26.5 us: body(): lax.all_gather(w_out[layer_idx], 'dp', axis=0, tiled=True)]
    all_gather x8 -> x0, waiting for transfers between devices: 64.7 us -> none  [the longest x2 49.9 us: layer_forward(): all_kv = lax.all_gather(local_kv, 'ctx', axis=0, tiled=True)]
    psum x0 -> x1, blocking collectives: none -> 64.2 us  [body(): ggs[l] = lax.psum(gg[:2], ('dp', 'ctx'))]
  transfers between devices with their start and end apart: 26 -> 0, of which waited for: 22 -> 0; matrix products, arithmetic and copies ran while one was open for 16% -> 0% of each run, Pallas kernels for 0% -> 0%
where the time goes in v1:
time: 417 us; the launch traced here: 416 us
  Pallas kernels  314 us (75%)
  blocking collectives  64.2 us (15%)
  local copies, waits for them, and re-layouts  24.1 us (6%)
  other arithmetic  12.3 us (3%)
    pallas_call x2, Pallas kernels, backward_layer(): pl.pallas_call(functools.partial(backward_kernel, layer), out_shape=(jax....  94.5 us
    pallas_call x1, Pallas kernels, reduce_grads(): pl.pallas_call(reduce_kernel, out_shape=jax.ShapeDtypeStruct((LAYERS, NX,...  90.6 us
    pallas_call x2, Pallas kernels, forward_layer(): pl.pallas_call(functools.partial(forward_kernel, layer), out_shape=(jax.S...  68.9 us
    psum x1, blocking collectives, body(): ggs[l] = lax.psum(gg[:2], ('dp', 'ctx'))  64.2 us
    pallas_call x1, Pallas kernels, gather_weights(): pl.pallas_call(weights_kernel, out_shape=(jax.ShapeDtypeStruct((LAYERS, N...  59.7 us

profile of v1, /device:TPU:1, one launch (start us, length us, event | category | flops | bytes accessed | tf_op | source)
XLA Modules:
  0.0 416.4 jit_solution(1384571620845934919)
XLA Ops:
  0.7 1.4 dynamic_slice.6
  4.5 1.3 select_bitcast_fusion.2
  7.6 1.5 scatter.9.gin
  9.1 1.1 copy.37
  12.8 1.8 copy.42.g_ref
  14.5 1.6 concatenate.20
  16.5 2.1 pad_maximum_fusion.win
  18.6 1.5 or_convert_fusion
  20.1 59.7 %gather_weights.1 = (bf16[2,4,4,4,144,384]{5,4,3,2,1,0:T(8,128)(2,1)}, bf16[4,16,256]{2,1,0:T(8,128)(2,1)}) custom-call(bf16[2,4,4,144,384]{4,3,2,1,0:T(8,128)(2,1)} %pad_maximum_fusion.win, bf16[16,256]{1,0:T(8,128)(2,1)} %copy-done.4), custom_call_target="tpu_custom_call" | custom-call | tf_op jit(solution)/shard_map/gather_weights/pallas_call | solution.py:351
  82.3 34.7 %forward_layer.2 = (f32[128,576]{1,0:T(8,128)}, f32[128,576]{1,0:T(8,128)}, bf16[128,640]{1,0:T(8,128)(2,1)}, bf16[3,384,256]{2,1,0:T(8,128)(2,1)}, bf16[4,4,2,6...) custom-call(f32[128,576]{1,0:T(8,128)} %convert_element_type.34.h_ref, ...), custom_call_target="tpu_custom_call" | custom-call | tf_op jit(solution)/shard_map/forward_layer/pallas_call | solution.py:521
  117.0 34.2 %forward_layer.3 = (f32[128,576]{1,0:T(8,128)}, f32[128,576]{1,0:T(8,128)}, bf16[128,640]{1,0:T(8,128)(2,1)}, bf16[3,384,256]{2,1,0:T(8,128)(2,1)}, bf16[4,4,2,6...) custom-call(f32[128,576]{1,0:T(8,128)} %get-tuple-element.59.h_ref, ...), custom_call_target="tpu_custom_call" | custom-call | tf_op jit(solution)/shard_map/forward_layer/pallas_call | solution.py:521
  151.2 1.0 convert_element_type.40
  152.2 0.8 copy.46
  153.0 46.0 %backward_layer.2 = (f32[128,576]{1,0:T(8,128)}, bf16[4,4,4,144,384]{4,3,2,1,0:T(8,128)(2,1)}, f32[8,576]{1,0:T(8,128)}) custom-call(f32[128,576]{1,0:T(8,128)} %copy.42.g_ref, f32[128,576]{1,0:T(8,128)} %get-tuple-element.59.h_ref, f32[128,576]{1,0:T(8,128)} %get-tuple-element.61.mid_ref, bf16[128,640]{1,0:T(8,128)(2,1)} %get-tuple-element.62.attn_ref, ...), custom_call_target="tpu_custom_call" | custom-call | tf_op jit(solution)/shard_map/backward_layer/pallas_call | solution.py:767
  199.0 48.4 %backward_layer.3 = (f32[128,576]{1,0:T(8,128)}, bf16[4,4,4,144,384]{4,3,2,1,0:T(8,128)(2,1)}, f32[8,576]{1,0:T(8,128)}) custom-call(f32[128,576]{1,0:T(8,128)} %get-tuple-element.67.g_ref, f32[128,576]{1,0:T(8,128)} %convert_element_type.34.h_ref, f32[128,576]{1,0:T(8,128)} %get-tuple-element.68.mid_ref, bf16[128,640]{1,0:T(8,128)(2,1)} %get-tuple-element.69.attn_ref, ...), custom_call_target="tpu_custom_call" | custom-call | tf_op jit(solution)/shard_map/backward_layer/pallas_call | solution.py:767
  247.5 90.6 %reduce_grads.1 = bf16[2,4,4,144,384]{4,3,2,1,0:T(8,128)(2,1)} custom-call(bf16[4,4,4,144,384]{4,3,2,1,0:T(8,128)(2,1)} %get-tuple-element.75.g0, bf16[4,4,4,144,384]{4,3,2,1,0:T(8,128)(2,1)} %get-tuple-element.76.g1), custom_call_target="tpu_custom_call" | custom-call | tf_op jit(solution)/shard_map/reduce_grads/pallas_call | solution.py:896
  338.1 2.0 copy.47
  341.5 64.2 %all-reduce.1 = (f32[2,1,576]{2,0,1:T(2,128)}, f32[2,1,576]{2,0,1:T(2,128)}) all-reduce(f32[2,1,576]{2,0,1:T(2,128)S(1)} %slice_bitcast_fusion.4, f32[2,1,576]{2,0,1:T(2,128)S(1)} %slice_bitcast_fusion.3), channel_id=1, replica_groups=mesh['dp'=4,'ctx'=32] {'dp','ctx'}, use_global_device_ids=true, to_apply=%region_0.1 | all-reduce | flops 2304 | bytes 18432 | tf_op jit(solution)/shard_map/psum | solution.py:995
  405.7 0.8 fusion.1
  407.6 2.5 slice.140
  411.1 1.4 copy.55
  412.6 1.4 copy.54
  414.2 0.9 fusion.4
  415.1 1.3 fusion.3
  (54 shorter events, 12.0 us)
Async XLA Ops:
  0.6 15.6 %copy-start.1 = (bf16[2,144,1536]{2,1,0:T(8,128)(2,1)S(1)}, bf16[2,144,1536]{2,1,0:T(8,128)(2,1)}, u32[]{:S(2)}) copy-start(bf16[2,144,1536]{2,1,0:T(8,128)(2,1)} %param.23) | copy-start | bytes 2654212
  0.7 15.5 %copy-start.2 = (bf16[2,144,1536]{2,1,0:T(8,128)(2,1)S(1)}, bf16[2,144,1536]{2,1,0:T(8,128)(2,1)}, u32[]{:S(2)}) copy-start(bf16[2,144,1536]{2,1,0:T(8,128)(2,1)} %param.22) | copy-start | bytes 2654212
  9.1 7.3 %copy-start.4 = (bf16[16,256]{1,0:T(8,128)(2,1)}, bf16[16,256]{1,0:T(8,128)(2,1)S(1)}, u32[]{:S(2)}) copy-start(bf16[16,256]{1,0:T(8,128)(2,1)S(1)} %scatter.9.gin) | copy-start | bytes 24580
  14.5 1.9 copy-start.3
  16.5 2.1 copy-start.5
  16.5 2.1 copy-start.6
  16.5 2.1 copy-start.7
  16.5 2.1 copy-start.8
  338.1 72.1 %copy-start = (bf16[2,4,4,144,384]{4,3,2,1,0:T(8,128)(2,1)S(1)}, bf16[2,4,4,144,384]{4,3,2,1,0:T(8,128)(2,1)}, u32[]{:S(2)}) copy-start(bf16[2,4,4,144,384]{4,3,2,1,0:T(8,128)(2,1)} %reduce_grads.1) | copy-start | bytes 10616836

commit v2 on v1

v2 whole, which is shorter than its diff:
```python
import functools

import jax
import jax.numpy as jnp
from jax import lax
from jax.experimental import pallas as pl
from jax.experimental.pallas import tpu as pltpu
from jax.sharding import PartitionSpec as P

HEADS = 9
KV = 3
HD = 64
LAYERS = 2
D = 576
FF = 1536
NX = 4
NZ = 4
NY = 4
NORM_EPS = 1e-05
ROPE_BASE = 100000.0
NEG = -1e30
BIG = 1e30
MESH = pl.DeviceIdType.MESH
ALL = slice(None)
F32 = jnp.float32
BF = jnp.bfloat16
VMEM_LIMIT = 60 * 1024 * 1024
DIRS = (2, 1, -1)
SEMS = 256


def place():
    ctx = lax.axis_index("ctx")
    return lax.div(ctx, 8), lax.rem(lax.div(ctx, 2), 4), lax.rem(ctx, 2)


def ctx_of(x, z, c):
    return (x * NZ + z) * 2 + c


def turn(i, d):
    return lax.rem(i + (d + 4), 4)


def neighbour(axis, d):
    x, z, c = place()
    return ctx_of(turn(x, d), z, c) if axis == 0 else ctx_of(x, turn(z, d), c)


def other_core():
    x, z, c = place()
    return ctx_of(x, z, 1 - c)


def greet(dp_too=False, far_too=False):
    barrier = pltpu.get_barrier_semaphore()
    x, z, c = place()
    ids = [neighbour(0, 1), neighbour(0, -1), neighbour(1, 1), neighbour(1, -1), other_core()]
    if far_too:
        ids += [neighbour(0, 2), neighbour(1, 2)]
    for i in ids:
        pl.semaphore_signal(barrier, inc=1, device_id={"ctx": i}, device_id_type=MESH)
    count = len(ids)
    if dp_too:
        y = lax.axis_index("dp")
        for k in (1, 2, 3):
            pl.semaphore_signal(barrier, inc=1, device_id={"dp": turn(y, k)}, device_id_type=MESH)
        count += 3
    pl.semaphore_wait(barrier, count)


class Wire:
    def __init__(self, send, recv):
        self.send, self.recv, self.open, self.used = send, recv, [], 0

    def take(self, n):
        self.used += n
        assert self.used <= SEMS
        return self.used - n

    def desc(self, src, dst, k, dev):
        return pltpu.make_async_remote_copy(
            src_ref=src,
            dst_ref=dst,
            send_sem=self.send.at[k],
            recv_sem=self.recv.at[k],
            device_id=dev,
            device_id_type=MESH,
        )

    def go(self, src, dst, k, dev):
        copy = self.desc(src, dst, k, dev)
        copy.start()
        self.open.append(copy)

    def got(self, dst, k, dev):
        self.desc(dst, dst, k, dev).wait_recv()

    def close(self):
        for copy in self.open:
            copy.wait_send()
        self.open = []


def lockstep(gens):
    gens = list(gens)
    while gens:
        left = []
        for g in gens:
            try:
                next(g)
                left.append(g)
            except StopIteration:
                pass
        gens = left
        yield


def run_all(gens):
    for _ in lockstep(gens):
        pass


def tick(gen):
    try:
        next(gen)
    except StopIteration:
        pass


def halves(h):
    x, z, _ = place()
    return ((0, 1), (x, z)) if h == 0 else ((1, 0), (z, x))


def xz(h, first, second):
    return (first, second) if h == 0 else (second, first)


def on_plane(axis, d):
    return {"ctx": neighbour(axis, d)}


def on_y(d):
    return {"dp": turn(lax.axis_index("dp"), d)}


def gather_half(wire, h, view, share_view):
    c = place()[2]
    axes, (me1, me2) = halves(h)
    oth = {"ctx": other_core()}
    near, far, core = wire.take(3), wire.take(12), wire.take(4)
    firsts = [me1] + [turn(me1, -d) for d in DIRS]

    def along(n):
        block = view(firsts[n], me2)
        for j, d in enumerate(DIRS):
            wire.go(block, block, far + 3 * n + j, on_plane(axes[1], d))

    own = view(me1, me2)
    for j, d in enumerate(DIRS):
        wire.go(own, own, near + j, on_plane(axes[0], d))
    along(0)
    yield
    for j in (1, 2, 0):
        wire.got(view(firsts[j + 1], me2), near + j, oth)
        along(j + 1)
    mine = share_view(ALL, me2, c)
    wire.go(mine, mine, core + 3, oth)
    yield
    for j in (1, 2, 0):
        second = turn(me2, -DIRS[j])
        for n in range(4):
            wire.got(view(firsts[n], second), far + 3 * n + j, oth)
        part = share_view(ALL, second, c)
        wire.go(part, part, core + j, oth)
    yield
    for j in range(4):
        second = turn(me2, -DIRS[j]) if j < 3 else me2
        wire.got(share_view(ALL, second, 1 - c), core + j, oth)


def add_into(dst, *srcs):
    if len(dst.shape) > 2:

        def step(i, carry):
            add_into(dst.at[i], *[s.at[i] for s in srcs])
            return carry

        if len(dst.shape) == 3:
            for i in range(dst.shape[0]):
                step(i, 0)
        else:
            lax.fori_loop(0, dst.shape[0], step, 0)
        return
    total = dst[...].astype(F32)
    for s in srcs:
        total = total + s[...].astype(F32)
    dst[...] = total.astype(dst.dtype)


def core_swap(wire, me, src, dst):
    base = wire.take(4)
    order = DIRS + (0,)
    oth = {"ctx": other_core()}
    for k, d in enumerate(order):
        wire.go(src(turn(me, d)), dst(turn(me, d)), base + k, oth)

    def ready_of(view):
        def ready(d):
            f = turn(me, d)
            wire.got(dst(f), base + order.index(d), oth)
            add_into(view(f), dst(f))

        return ready

    return ready_of


def ring_reduce(wire, me, dev, at, buf, ready):
    base = wire.take(3)
    for j, d in enumerate(DIRS):
        ready(d)
        wire.go(at(turn(me, d)), buf.at[j], base + j, dev(d))
    ready(0)
    yield
    for j, d in enumerate(DIRS):
        wire.got(buf.at[j], base + j, dev(d))
    add_into(at(me), buf.at[0], buf.at[1], buf.at[2])


def scatter_half(wire, h, view, bufs, ready):
    axes, pos = halves(h)
    yield from ring_reduce(
        wire, pos[0], lambda d: on_plane(axes[0], d), lambda i: view(i, ALL), bufs[0], ready
    )
    yield from ring_reduce(
        wire, pos[1], lambda d: on_plane(axes[1], d), lambda i: view(pos[0], i), bufs[1],
        lambda d: None,
    )


def lanes(shape):
    return lax.broadcasted_iota(jnp.int32, shape, len(shape) - 1)


def mm(a, b):
    return lax.dot_general(a, b, (((1,), (0,)), ((), ())), preferred_element_type=F32)


def mm_t(a, b):
    return lax.dot_general(a, b, (((1,), (1,)), ((), ())), preferred_element_type=F32)


def tmm(a, b):
    return lax.dot_general(a, b, (((0,), (0,)), ((), ())), preferred_element_type=F32)


def inv_rms(v):
    return lax.rsqrt(jnp.mean(v * v, axis=-1, keepdims=True) + NORM_EPS)


def norm_back(v, g, d):
    r = inv_rms(v)
    dv = r * g * d - v * (r * r * r * jnp.mean(g * d * v, axis=-1, keepdims=True))
    return dv, jnp.sum(d * v * r, axis=0, keepdims=True)


def rope(t, cos, ssin):
    first = lax.rem(lanes(t.shape), HD) < HD // 2
    turned = jnp.where(first, pltpu.roll(t, 96, 1), pltpu.roll(t, 32, 1))
    return t * cos + turned * ssin


def pair(t, half):
    lo, hi = t[:64], t[64:]
    first = lanes((64, 128)) < HD
    if half == 0:
        return jnp.where(first, lo, pltpu.roll(hi, HD, 1))
    return jnp.where(first, pltpu.roll(lo, HD, 1), hi)


def unpair(a, b):
    first = lanes((64, 128)) < HD
    lo = jnp.where(first, a, pltpu.roll(b, HD, 1))
    hi = jnp.where(first, pltpu.roll(a, HD, 1), b)
    return jnp.concatenate([lo, hi], axis=0)


def tile(v, i):
    return v[:, 128 * i : 128 * i + 128]


def doubled(p):
    first = lanes((192, 128)) < HD
    one = jnp.where(first, pltpu.roll(p, HD, 1), 0.0)
    zero = jnp.zeros((192, 128), F32)
    return jnp.concatenate(
        [jnp.concatenate([one, zero], axis=1), jnp.concatenate([zero, p], axis=1)], axis=0
    ).astype(BF)


def slot_row(scal, c, row_a, row_b):
    pick = jnp.full((1, 384), scal[2, c], F32) > 0.5
    own = jnp.full((1, 384), scal[3, c], F32)
    extra = jnp.where(lanes((1, 384)) >= 192, own, 0.0)
    return jnp.where(pick, row_a, row_b), extra


def rel(i):
    return turn(i - lax.axis_index("dp"), 4)


def w_mat(wv, kind, i):
    return jnp.concatenate([wv[kind, i, rel(j)] for j in range(NY)], axis=0)


def w_attn(wa, i):
    return jnp.concatenate([wa[i, rel(j)] for j in range(NY)], axis=0)


def w_down(wv, i):
    return wv[3, :, rel(i)].reshape(D, 384)


def load_weights(w_attn_any, w_mlp_any, wa, wm, sems):
    return [
        pltpu.make_async_copy(w_mlp_any.at[0], wm.at[0], sems.at[0]),
        pltpu.make_async_copy(w_mlp_any.at[1], wm.at[1], sems.at[1]),
        pltpu.make_async_copy(w_attn_any, wa, sems.at[2]),
        pltpu.make_async_copy(w_mlp_any.at[3], wm.at[3], sems.at[3]),
    ]


def multiple(v, n):
    return pl.multiple_of(v, n)


def kv_gather(wire, kv, k):
    c = place()[2]

    def gen(h):
        def view(first, second):
            xi, zi = xz(h, first, second)
            return kv.at[xi, zi, c, k, h]

        def share(first, second, core):
            xi, zi = xz(h, first, second)
            return kv.at[xi, zi, core, k, h]

        return gather_half(wire, h, view, share)

    return lockstep([gen(h) for h in (0, 1)])


def chunk_of(buf, ci, k, j):
    return buf[ci // 2, pl.ds(2 * (ci % 2), 2), :, k, j].reshape(256, 128)


def diag_keys(k):
    first = lanes((64, 128)) < HD
    zero = jnp.zeros((64, 128), k.dtype)
    both = jnp.concatenate([jnp.where(first, k, zero), jnp.where(first, zero, k)], axis=0)
    return both


def diag_bias():
    shape = (128, 384)
    key = lax.rem(lax.broadcasted_iota(jnp.int32, shape, 0), 64)
    q = lanes(shape)
    visible = (q >= 192) & (key <= lax.rem(q, 64))
    return jnp.where(visible, 0.0, NEG)


def row_split():
    c = place()[2]
    mine = pl.ds(multiple(64 * c, 16), 80)
    return mine, lambda core: pl.ds(multiple(80 * core, 16), 64)


def over_y(wire, src, view):
    mine, handed = row_split()
    c = place()[2]
    oth = {"ctx": other_core()}
    near, core = wire.take(3), wire.take(3)
    for j, d in enumerate(DIRS):
        wire.go(src(mine), view((4 - d) % 4, mine), near + j, on_y(d))
    yield
    for j in (1, 2, 0):
        k = (4 - DIRS[j]) % 4
        wire.got(view(k, mine), near + j, oth)
        part = view(k, handed(c))
        wire.go(part, part, core + j, oth)
    yield
    for j in range(3):
        wire.got(view((4 - DIRS[j]) % 4, handed(1 - c)), core + j, oth)


def attn_weights_gen(wire, win, wa, first, count):
    blocks = pl.ds(first, count)
    return over_y(
        wire, lambda rows: win.at[blocks, rows], lambda k, rows: wa.at[blocks, k, rows]
    )


def weights_gen(wire, win, w, own):
    x, z, _ = place()
    mine, handed = row_split()
    hi, lo = pl.ds(256, 128), pl.ds(0, 256)
    own.start()
    around = over_y(
        wire, lambda rows: win.at[:, :, rows, hi], lambda k, rows: w.at[:, :, k, rows, hi]
    )

    def over():
        near = wire.take(3)
        for j, d in enumerate(DIRS):
            wire.go(
                win.at[x, z, mine, lo], w.at[x, z, (4 - d) % 4, mine, lo], near + j, on_y(d)
            )
        yield
        for j, d in enumerate(DIRS):
            wire.got(w.at[x, z, (4 - d) % 4, mine, lo], near + j, on_y(d))

        def half(h):
            cols = pl.ds(128 * h, 128)

            def view(first, second):
                xi, zi = xz(h, first, second)
                return w.at[xi, zi, pl.ds(1, 3), mine, cols]

            def share(first, second, core):
                xi, zi = xz(h, first, second)
                return w.at[xi, zi, pl.ds(1, 3), handed(core), cols]

            return gather_half(wire, h, view, share)

        yield from lockstep([half(0), half(1)])

    yield from lockstep([over(), around])
    own.wait()


def gains_exchange(wire, gin, landing):
    base = wire.take(3)
    for j, d in enumerate(DIRS):
        wire.go(gin, landing.at[(4 - d) % 4], base + j, on_y(d))
    yield
    for j, d in enumerate(DIRS):
        wire.got(landing.at[(4 - d) % 4], base + j, on_y(d))


def gains_rows(gin, landing):
    total = jnp.zeros((16, 640), F32)
    landing[0] = gin[...]
    for j in range(NY):
        part = landing[rel(j)].astype(F32)
        part = jnp.concatenate([part, jnp.zeros((16, 384), F32)], axis=1)
        total = total + (pltpu.roll(part, 144 * j, 1) if j else part)
    return total


def first_forward_kernel(
    h_ref, win_a, win_b, gin, cos_ref, sin_ref, mask_ref, ind_ref, scal,
    next_ref, mid_ref, attn_ref, qt_ref, kv, lse_ref, op_ref, a_out, b_out, gains,
    wa, wm, s_scr, sd_scr, acc_scr, landing, send, recv, loc,
):
    greet(True, True)
    wire = Wire(send, recv)
    own_a = pltpu.make_async_copy(win_a, wa.at[:, 0], loc.at[0])
    own_b = pltpu.make_async_copy(win_b, wm.at[:, :, 0], loc.at[1])
    own_a.start()
    early = attn_weights_gen(wire, win_a, wa, 0, 3)
    tick(early)
    last = attn_weights_gen(wire, win_a, wa, 3, 1)
    run_all([early, gains_exchange(wire, gin, landing), last])
    own_a.wait()
    keep_a = pltpu.make_async_copy(wa, a_out, loc.at[2])
    keep_a.start()
    gains[...] = gains_rows(gin, landing)
    later = weights_gen(wire, win_b, wm, own_b)
    tick(later)

    def need(kind):
        if kind == 0:
            run_all([later])

    forward_core(
        0, wire, later, need, h_ref, gains, cos_ref, sin_ref, mask_ref, ind_ref, scal,
        next_ref, mid_ref, attn_ref, qt_ref, kv, lse_ref, op_ref, wa, wm, s_scr, sd_scr, acc_scr,
    )
    keep_b = pltpu.make_async_copy(wm, b_out, loc.at[3])
    keep_b.start()
    keep_a.wait()
    keep_b.wait()
    wire.close()


def second_forward_kernel(
    h_ref, b_any, win_m, gains, cos_ref, sin_ref, mask_ref, ind_ref, scal,
    next_ref, mid_ref, attn_ref, qt_ref, kv, lse_ref, op_ref, m_out,
    wa, wm, s_scr, sd_scr, acc_scr, send, recv, loc,
):
    load = pltpu.make_async_copy(b_any.at[2], wa, loc.at[0])
    load.start()
    greet(True, True)
    wire = Wire(send, recv)
    later = weights_gen(wire, win_m, wm, pltpu.make_async_copy(win_m, wm.at[:, :, 0], loc.at[1]))
    tick(later)

    def need(kind):
        if kind == 2:
            load.wait()
        if kind == 0:
            run_all([later])

    forward_core(
        1, wire, later, need, h_ref, gains, cos_ref, sin_ref, mask_ref, ind_ref, scal,
        next_ref, mid_ref, attn_ref, qt_ref, kv, lse_ref, op_ref, wa, wm, s_scr, sd_scr, acc_scr,
    )
    keep = pltpu.make_async_copy(wm, m_out, loc.at[2])
    keep.start()
    keep.wait()
    wire.close()


def forward_core(
    layer, wire, later, need, h_ref, gains, cos_ref, sin_ref, mask_ref, ind_ref, scal,
    next_ref, mid_ref, attn_ref, qt_ref, kv, lse_ref, op_ref, wa, wm, s_scr, sd_scr, acc_scr,
):
    x, z, c = place()
    h = h_ref[...]
    n1 = (h * inv_rms(h) * gains[layer : layer + 1, :D]).astype(BF)
    need(2)
    cos, ssin = cos_ref[...], sin_ref[...]
    low = lanes((128, 128)) < HD
    kv_part = mm(n1, w_attn(wa, 0))
    t0, t1, t2 = [tile(kv_part, i) for i in range(3)]
    t0 = rope(t0, cos, ssin)
    t1 = jnp.where(low, rope(t1, cos, ssin), t1)
    k_pairs = [pair(t0, 0), pair(t0, 1), pair(t1, 0)]
    v_pairs = [pair(t1, 1), pair(t2, 0), pair(t2, 1)]
    spread = []
    for k in range(KV):
        kv[x, z, c, k, 0] = k_pairs[k].astype(BF)
        kv[x, z, c, k, 1] = v_pairs[k].astype(BF)
        spread.append(kv_gather(wire, kv, k))
        tick(spread[k])
    q_part = [mm(n1, w_attn(wa, i)) for i in (1, 2)]
    tiles = [rope(tile(q_part[i // 3], i % 3), cos, ssin) for i in range(5)]
    for k in range(KV):
        qp = jnp.concatenate(
            [pair(tiles[(3 * k + g) // 2], (3 * k + g) % 2) for g in range(3)], axis=0
        )
        qt_ref[k] = doubled(qp * 0.125)

    in_one = lanes((1, 384)) < 192
    bias = diag_bias()
    zero128 = jnp.zeros((128, 128), BF)
    runs = []
    for k in range(KV):
        keys = diag_keys(kv[x, z, c, k, 0])
        sd = mm_t(jnp.concatenate([zero128, keys], axis=1), qt_ref[k]) + bias
        sd_scr[k] = sd
        lo = jnp.max(sd[:64].reshape(8, 8, 384), axis=0)
        hi = jnp.max(sd[64:].reshape(8, 8, 384), axis=0)
        runs.append((jnp.full((8, 384), NEG, F32), lo, hi))
    dlane = lanes((128, 128))
    drow = lax.broadcasted_iota(jnp.int32, (128, 128), 0)
    dind = jnp.where(
        ((dlane == 65) & (drow < 64)) | ((dlane == 66) & (drow >= 64)), 1.0, 0.0
    ).astype(BF)
    first = lanes((256, 128)) < HD

    def scores(k):
        def step(pairi, carry):
            one, lo, hi = carry
            for ci in (2 * pairi, 2 * pairi + 1):
                keys = chunk_of(kv, ci, k, 0)
                s = mm_t(jnp.concatenate([keys, keys * mask_ref[ci]], axis=1), qt_ref[k])
                s_scr[k, ci] = s
                for i in range(4):
                    top = jnp.max(s[64 * i : 64 * i + 64].reshape(8, 8, 384), axis=0)
                    slot = 4 * ci + i
                    one = jnp.maximum(one, top)
                    lo = jnp.maximum(lo, top + scal[0, slot])
                    hi = jnp.maximum(hi, top + scal[1, slot])
            return one, lo, hi

        got = lax.fori_loop(0, 4, step, runs[k])
        one, lo, hi = [jnp.max(r, axis=0, keepdims=True) for r in got]
        top = jnp.where(in_one, one, hi)
        top = jnp.maximum(top, pltpu.roll(top, 192, 1))
        return jnp.where(in_one, top, lo), top

    def values(k, row_a, row_b):
        sd = sd_scr[k]
        p = jnp.concatenate([jnp.exp(sd[:64] - row_a), jnp.exp(sd[64:] - row_b)], axis=0)
        vals = jnp.concatenate([dind, diag_keys(kv[x, z, c, k, 1])], axis=1)
        acc_scr[k] = tmm(vals, p.astype(BF))

        def step(pairi, carry):
            total = acc_scr[k]
            for ci in (2 * pairi, 2 * pairi + 1):
                s = s_scr[k, ci]
                parts = []
                for i in range(4):
                    base, extra = slot_row(scal, 4 * ci + i, row_a, row_b)
                    parts.append(jnp.exp(s[64 * i : 64 * i + 64] - (base + extra)))
                p = jnp.concatenate(parts, axis=0).astype(BF)
                v = chunk_of(kv, ci, k, 1)
                vals = jnp.concatenate(
                    [jnp.where(first, v, ind_ref[ci]), v * mask_ref[ci]], axis=1
                )
                total = total + tmm(vals, p)
            acc_scr[k] = total
            return carry

        lax.fori_loop(0, 4, step, 0)

    for k in range(KV):
        tick(spread[k])
    tick(later)
    row_a, row_b = [], []
    run_all([spread[0]])
    for k in range(KV):
        if k + 1 < KV:
            tick(spread[k + 1])
        tick(later)
        a, b = scores(k)
        row_a.append(a)
        row_b.append(b)
        if k + 1 < KV:
            run_all([spread[k + 1]])
        values(k, a, b)

    pairs = []
    for k in range(KV):
        acc = acc_scr[k]
        rolled = pltpu.roll(acc, 192, 1)
        hi = acc[0:64] + rolled[192:256]
        lo = rolled[128:192]
        tot_hi = acc[64:65] + rolled[66:67]
        tot_lo = rolled[65:66]
        lse_hi = row_b[k] + jnp.log(jnp.where(in_one, tot_hi, 1.0))
        lse_hi = jnp.where(in_one, lse_hi, pltpu.roll(lse_hi, 192, 1))
        lse_lo = pltpu.roll(row_a[k], 192, 1) + jnp.log(jnp.where(in_one, tot_lo, 1.0))
        lse_ref[k, 0:1] = jnp.where(in_one, lse_hi, pltpu.roll(lse_lo, 192, 1))
        lse_ref[k, 1:2] = lse_hi
        lse_ref[k, 2:8] = jnp.zeros((6, 384), F32)
        out_t = jnp.concatenate(
            [lo / jnp.where(in_one, tot_lo, 1.0), hi / jnp.where(in_one, tot_hi, 1.0)], axis=0
        )
        p = jnp.transpose(out_t)[:192]
        op_ref[k] = p
        pairs += [p[64 * g : 64 * g + 64] for g in range(3)]
    pairs.append(jnp.zeros((64, 128), F32))
    attn = jnp.concatenate(
        [unpair(pairs[2 * t], pairs[2 * t + 1]) for t in range(5)], axis=1
    ).astype(BF)
    attn_ref[...] = attn
    a = attn[:, :D]
    proj = jnp.concatenate([mm(a, w_attn(wa, 2)), mm(a, w_attn(wa, 3))], axis=1)
    mid = h + pltpu.roll(proj, D, 1)[:, :D]
    mid_ref[...] = mid
    n2 = (mid * inv_rms(mid) * gains[2 + layer : 3 + layer, :D]).astype(BF)
    need(0)
    for i in range(4):
        gate = mm(n2, w_mat(wm, 0, i))
        up = mm(n2, w_mat(wm, 1, i))
        inner = (gate * jax.nn.sigmoid(gate) * up).astype(BF)
        mid = mid + mm_t(inner, w_down(wm, i))
    next_ref[...] = mid


SAVED = (
    jax.ShapeDtypeStruct((128, D), F32),
    jax.ShapeDtypeStruct((128, D), F32),
    jax.ShapeDtypeStruct((128, 640), BF),
    jax.ShapeDtypeStruct((KV, 384, 256), BF),
    jax.ShapeDtypeStruct((NX, NZ, 2, KV, 2, 64, 128), BF),
    jax.ShapeDtypeStruct((KV, 8, 384), F32),
    jax.ShapeDtypeStruct((KV, 192, 128), F32),
)
FORWARD_SCRATCH = (
    ((4, 4, 144, 384), BF),
    ((4, 4, 4, 144, 384), BF),
    ((KV, 8, 256, 384), F32),
    ((KV, 128, 384), F32),
    ((KV, 256, 384), F32),
)
GATHERED = jax.ShapeDtypeStruct((NX, NZ, NY, 144, 384), BF)
ATTN_GATHERED = jax.ShapeDtypeStruct((4, NY, 144, 384), BF)


def specs():
    return (
        pl.BlockSpec(memory_space=pltpu.VMEM),
        pl.BlockSpec(memory_space=pl.ANY),
        pl.BlockSpec(memory_space=pltpu.SMEM),
    )


def sems(*counts):
    return [pltpu.SemaphoreType.DMA((n,)) for n in counts]


def params(cid):
    return pltpu.CompilerParams(
        collective_id=cid, has_side_effects=True, vmem_limit_bytes=VMEM_LIMIT
    )


def first_forward(h, win_a, win_b, gin, cos, ssin, mask, ind, scal):
    vm, anyw, sm = specs()
    return pl.pallas_call(
        first_forward_kernel,
        out_shape=SAVED + (ATTN_GATHERED, GATHERED, jax.ShapeDtypeStruct((16, 640), F32)),
        in_specs=[vm, anyw, anyw, vm, vm, vm, vm, vm, sm],
        out_specs=(vm,) * 7 + (anyw, anyw, vm),
        scratch_shapes=[pltpu.VMEM(*v) for v in FORWARD_SCRATCH]
        + [pltpu.VMEM((NY, 16, 256), BF)]
        + sems(SEMS, SEMS, 4),
        compiler_params=params(0),
        name="first_forward",
    )(h, win_a, win_b, gin, cos, ssin, mask, ind, scal)


def second_forward(h, w_b, win_m, gains, cos, ssin, mask, ind, scal):
    vm, anyw, sm = specs()
    return pl.pallas_call(
        second_forward_kernel,
        out_shape=SAVED + (GATHERED,),
        in_specs=[vm, anyw, anyw, vm, vm, vm, vm, vm, sm],
        out_specs=(vm,) * 7 + (anyw,),
        scratch_shapes=[pltpu.VMEM(*v) for v in FORWARD_SCRATCH] + sems(SEMS, SEMS, 3),
        compiler_params=params(1),
        name="second_forward",
    )(h, w_b, win_m, gains, cos, ssin, mask, ind, scal)


def transposed(v, wide):
    wide[:, :D] = v.astype(F32)
    return jnp.transpose(wide[...])[:D].astype(BF)


def first_backward_kernel(*refs):
    ins, attn_any, mlp_any = refs[:13], refs[13], refs[14]
    dh_ref, g_attn, gg_ref, summed = refs[15:19]
    work, rest = refs[19 : 19 + N_WORK], refs[19 + N_WORK :]
    gm, bufs, (send, recv, loc) = rest[0], rest[1:-3], rest[-3:]
    loads = load_weights(attn_any, mlp_any, work[0], work[1], loc)
    for k in (0, 1, 3, 2):
        loads[k].start()
    greet(True, True)
    wire = Wire(send, recv)
    gm[2] = jnp.zeros((4, 4, 144, 384), BF)
    batch = reduce_gen(wire, gm, summed, bufs, loc.at[4])
    backward_core(1, wire, batch, loads, ins, dh_ref, gm, g_attn, gg_ref, work)
    run_all([batch])
    wire.close()


def second_backward_kernel(*refs):
    ins, attn_any, mlp_any, ga1, gg1 = refs[:13], refs[13], refs[14], refs[15], refs[16]
    dh_ref, summed, summed_a, gains_out = refs[17:21]
    work, rest = refs[21 : 21 + N_WORK], refs[21 + N_WORK :]
    gm, ga, gg, steps, got = rest[:5]
    bufs, late = rest[5 : 5 + N_REDUCE], rest[5 + N_REDUCE : -3]
    send, recv, loc = rest[-3:]
    loads = load_weights(attn_any, mlp_any, work[0], work[1], loc)
    for k in (0, 1, 3, 2):
        loads[k].start()
    other = pltpu.make_async_copy(ga1, gm.at[2], loc.at[5])
    other.start()
    greet(True, True)
    wire = Wire(send, recv)
    batch = reduce_gen(wire, gm, summed, bufs, loc.at[4])
    other.wait()
    backward_core(0, wire, batch, loads, ins, dh_ref, gm, ga, gg, work)
    steps[0] = jnp.zeros((8, 640), F32)
    steps[0, 0:2, :D] = gg[0:2]
    steps[0, 2:4, :D] = gg1[0:2]
    run_all([attn_reduce_gen(wire, ga, summed_a, late), gains_gen(wire, steps, got), batch])
    gains_out[...] = steps[4]
    wire.close()


def backward_core(layer, wire, batch, loads, ins, dh_ref, gm, ga, gg_ref, work):
    (
        g_ref, h_ref, mid_ref, attn_ref, qt_ref, kv, lse_ref, op_ref, gains,
        cos_ref, sin_ref, mask_ref, scal,
    ) = ins
    wa, wm, dot_scr, dq_scr, pbuf, rcore, kv_one, kv_two, wide = work
    x, z, c = place()
    wide[...] = jnp.zeros((128, 640), F32)
    g = g_ref[...]
    mid = mid_ref[...]
    gain2 = gains[2 + layer : 3 + layer, :D]
    n2 = (mid * inv_rms(mid) * gain2).astype(BF)
    n2_t = transposed(n2, wide)
    branch = g.astype(BF)
    branch_t = transposed(branch, wide)
    d_n2 = jnp.zeros((128, D), F32)
    for k in (0, 1, 3):
        loads[k].wait()
    for i in range(4):
        gate_w, up_w, down_w = w_mat(wm, 0, i), w_mat(wm, 1, i), w_down(wm, i)
        gate = mm(n2, gate_w)
        up = mm(n2, up_w)
        sig = jax.nn.sigmoid(gate)
        act = gate * sig
        inner = (act * up).astype(BF)
        d_inner = mm(branch, down_w)
        d_gate = (d_inner * up * (sig + act * (1.0 - sig))).astype(BF)
        d_up = (d_inner * act).astype(BF)
        gm[0, i] = mm(n2_t, d_gate).astype(BF).reshape(4, 144, 384)
        gm[1, i] = mm(n2_t, d_up).astype(BF).reshape(4, 144, 384)
        gm[3, :, i] = mm(branch_t, inner).astype(BF).reshape(4, 144, 384)
        d_n2 = d_n2 + mm_t(d_gate, gate_w) + mm_t(d_up, up_w)
    tick(batch)
    d_hn, gg2 = norm_back(mid, gain2, d_n2)
    d_mid = g + d_hn
    gg_ref[1:2] = gg2
    gg_ref[2:8] = jnp.zeros((6, D), F32)
    loads[2].wait()
    wide[:, :D] = d_mid
    dm = jnp.concatenate([wide[...], jnp.zeros((128, 128), F32)], axis=1)
    dm = pltpu.roll(dm, 192, 1).astype(BF)
    d_attn = mm_t(dm[:, :384], w_attn(wa, 2)) + mm_t(dm[:, 384:], w_attn(wa, 3))
    wide[:, :D] = d_attn
    attn_t = jnp.transpose(attn_ref[...].astype(F32))[:D].astype(BF)
    g_out = mm(attn_t, dm)
    ga[3] = g_out[:, 384:].astype(BF).reshape(4, 144, 384)
    ga[2] = g_out[:, :384].astype(BF).reshape(4, 144, 384)
    da = wide[...].astype(BF).astype(F32)
    da_tiles = [tile(da, i) for i in range(5)]
    tick(batch)

    in_one = lanes((1, 384)) < 192
    pick_lo = jnp.where(
        lanes((16, 128)) < HD,
        jnp.where(lax.broadcasted_iota(jnp.int32, (16, 128), 0) == 0, 1.0, 0.0),
        jnp.where(lax.broadcasted_iota(jnp.int32, (16, 128), 0) == 1, 1.0, 0.0),
    ).astype(BF)
    delta_a, delta_b = [], []
    for k in range(KV):
        dp = jnp.concatenate(
            [pair(da_tiles[(3 * k + q) // 2], (3 * k + q) % 2) for q in range(3)], axis=0
        )
        dot_scr[k] = doubled(dp)
        prod = dp * op_ref[k]
        prod = jnp.concatenate([prod, prod], axis=0)
        coarse = prod.astype(BF)
        fine = (prod - coarse.astype(F32)).astype(BF)
        rows = mm_t(pick_lo, coarse) + mm_t(pick_lo, fine)
        lo, hi = rows[0:1], rows[1:2]
        delta_a.append(jnp.where(in_one, hi, lo))
        delta_b.append(hi)

    def back(k, keys2, vals2, subs, deltas, bias):
        s = mm_t(keys2, qt_ref[k])
        if bias is not None:
            s = s + bias
        dp = mm_t(vals2, dot_scr[k])
        probs, d_s = [], []
        for i, (sub, delta) in enumerate(zip(subs, deltas)):
            p = jnp.exp(s[64 * i : 64 * i + 64] - sub)
            probs.append(p.astype(BF))
            d_s.append((p * (dp[64 * i : 64 * i + 64] - delta)).astype(BF))
        probs = jnp.concatenate(probs, axis=0)
        d_s = jnp.concatenate(d_s, axis=0)
        return mm(d_s, qt_ref[k]), mm(probs, dot_scr[k]), tmm(keys2, d_s)

    bias = diag_bias()
    zero128 = jnp.zeros((128, 128), BF)
    first = lanes((64, 128)) < HD
    wide_first = lanes((256, 128)) < HD

    def head(k):
        own = []
        dk, dv, dq = back(
            k,
            jnp.concatenate([zero128, diag_keys(kv[x, z, c, k, 0])], axis=1),
            jnp.concatenate([zero128, diag_keys(kv[x, z, c, k, 1])], axis=1),
            [lse_ref[k, 0:1], lse_ref[k, 1:2]],
            [delta_a[k], delta_b[k]],
            bias,
        )
        for d in (dk, dv):
            own.append(jnp.where(first, d[:64, 128:], d[64:, 128:]))
        dq_scr[k] = dq

        def step(pairi, carry):
            total = dq_scr[k]
            for ci in (2 * pairi, 2 * pairi + 1):
                m = mask_ref[ci]
                keys, vals = chunk_of(kv, ci, k, 0), chunk_of(kv, ci, k, 1)
                subs, deltas = [], []
                for i in range(4):
                    base, extra = slot_row(scal, 4 * ci + i, lse_ref[k, 0:1], lse_ref[k, 1:2])
                    subs.append(base + extra)
                    deltas.append(slot_row(scal, 4 * ci + i, delta_a[k], delta_b[k])[0])
                dk, dv, dq = back(
                    k,
                    jnp.concatenate([keys, keys * m], axis=1),
                    jnp.concatenate([vals, vals * m], axis=1),
                    subs,
                    deltas,
                    None,
                )
                mf = m.astype(F32)
                for j, d in enumerate((dk, dv)):
                    both = jnp.where(wide_first, d[:, :128], 0.0) + mf * d[:, 128:]
                    both = both.astype(BF).reshape(2, 2, 64, 128)
                    pbuf[pairi, pl.ds(2 * (ci - 2 * pairi), 2), :, k, j] = both
                total = total + dq
            dq_scr[k] = total
            return carry

        lax.fori_loop(0, 2, step, 0)
        tick(batch)
        lax.fori_loop(2, 4, step, 0)
        for j in (0, 1):
            part = pbuf.at[x, z, c, k, j]
            part[...] = (part[...].astype(F32) + own[j]).astype(BF)

    def kv_reduce(k, h):
        me = halves(h)[1][0]

        def view(f, s):
            xi, zi = xz(h, f, s)
            return pbuf.at[xi, zi, c, k, h]

        def src(f):
            xi, zi = xz(h, f, ALL)
            return pbuf.at[xi, zi, 1 - c, k, h]

        def dst(f):
            xi, zi = xz(h, f, ALL)
            return rcore.at[xi, zi, k, h]

        ready_of = core_swap(wire, me, src, dst)
        return scatter_half(
            wire, h, view, (kv_one.at[k, h], kv_two.at[k, h]), ready_of(lambda f: view(f, ALL))
        )

    sums = []
    for k in range(KV):
        head(k)
        tick(batch)
        sums.append(lockstep([kv_reduce(k, j) for j in (0, 1)]))
        for gen in sums:
            tick(gen)

    h = h_ref[...]
    gain1 = gains[layer : layer + 1, :D]
    n1 = (h * inv_rms(h) * gain1).astype(BF)
    n1_t = transposed(n1, wide)
    cos, ssin = cos_ref[...], -sin_ref[...]
    pairs = []
    for k in range(KV):
        dq = dq_scr[k]
        rolled = pltpu.roll(dq, 192, 1)
        out_t = jnp.concatenate([rolled[128:192], dq[0:64] + rolled[192:256]], axis=0)
        p = jnp.transpose(out_t)[:192]
        pairs += [p[64 * q : 64 * q + 64] for q in range(3)]
    pairs.append(jnp.zeros((64, 128), F32))
    q_tiles = [
        (rope(unpair(pairs[2 * t], pairs[2 * t + 1]), cos, ssin) * 0.125).astype(BF)
        for t in range(5)
    ]
    q_tiles.append(jnp.zeros((128, 128), BF))
    d_n1 = jnp.zeros((128, D), F32)

    def attn_block(i, d):
        grad = mm(n1_t, d)
        if i == 2:
            grad = grad + ga[2].reshape(D, 384).astype(F32)
        ga[i] = grad.astype(BF).reshape(4, 144, 384)
        return mm_t(d, w_attn(wa, i))

    for i in (1, 2):
        d_n1 = d_n1 + attn_block(i, jnp.concatenate(q_tiles[3 * i - 3 : 3 * i], axis=1))
    tick(batch)
    run_all(sums)
    done = [[pbuf[x, z, c, k, j].astype(F32) for j in (0, 1)] for k in range(KV)]
    low = lanes((128, 128)) < HD
    t0 = rope(unpair(done[0][0], done[1][0]), cos, ssin)
    t1 = unpair(done[2][0], done[0][1])
    t1 = jnp.where(low, rope(t1, cos, ssin), t1)
    t2 = unpair(done[1][1], done[2][1])
    d_n1 = d_n1 + attn_block(0, jnp.concatenate([t0, t1, t2], axis=1).astype(BF))
    d_h, gg1 = norm_back(h, gain1, d_n1)
    gg_ref[0:1] = gg1
    dh_ref[...] = d_mid + d_h


BACKWARD_SCRATCH = (
    ((4, 4, 144, 384), BF),
    ((4, 4, 4, 144, 384), BF),
    ((KV, 384, 256), BF),
    ((KV, 256, 384), F32),
    ((NX, NZ, 2, KV, 2, 64, 128), BF),
    ((NX, NZ, KV, 2, 64, 128), BF),
    ((KV, 2, 3, 4, 64, 128), BF),
    ((KV, 2, 3, 64, 128), BF),
    ((128, 640), F32),
)
N_WORK = len(BACKWARD_SCRATCH)
SUMMED = jax.ShapeDtypeStruct((NX, NZ, 144, 384), BF)


def vmems(shapes):
    return [pltpu.VMEM(v, BF) for v in shapes]


def first_backward(ins):
    vm, anyw, sm = specs()
    return pl.pallas_call(
        first_backward_kernel,
        out_shape=(
            jax.ShapeDtypeStruct((128, D), F32), ATTN_GATHERED, jax.ShapeDtypeStruct((8, D), F32),
            SUMMED,
        ),
        in_specs=[vm] * 12 + [sm, anyw, anyw],
        out_specs=(vm,) * 4,
        scratch_shapes=[pltpu.VMEM(*v) for v in BACKWARD_SCRATCH]
        + [pltpu.VMEM((4, 4, 4, 144, 384), BF)] + vmems(REDUCE_SHAPES) + sems(SEMS, SEMS, 5),
        compiler_params=params(2),
        name="first_backward",
    )(*ins)


def second_backward(ins, ga1, gg1):
    vm, anyw, sm = specs()
    scratch = [pltpu.VMEM(*v) for v in BACKWARD_SCRATCH]
    scratch += [
        pltpu.VMEM((4, 4, 4, 144, 384), BF),
        pltpu.VMEM((4, 4, 144, 384), BF),
        pltpu.VMEM((8, D), F32),
        pltpu.VMEM((5, 8, 640), F32),
        pltpu.VMEM((10, 8, 640), F32),
    ]
    scratch += vmems(REDUCE_SHAPES) + vmems(ATTN_REDUCE_SHAPES)
    return pl.pallas_call(
        second_backward_kernel,
        out_shape=(
            jax.ShapeDtypeStruct((128, D), F32), SUMMED,
            jax.ShapeDtypeStruct((4, 144, 384), BF), jax.ShapeDtypeStruct((8, 640), F32),
        ),
        in_specs=[vm] * 12 + [sm, anyw, anyw, anyw, vm],
        out_specs=(vm,) * 4,
        scratch_shapes=scratch + sems(SEMS, SEMS, 6),
        compiler_params=params(3),
        name="second_backward",
    )(*ins, ga1, gg1)


REDUCE_SHAPES = (
    ((4, 4, 4, 80, 384),) * 2
    + ((3, 4, 2, 80, 256), (3, 2, 80, 256)) * 2
    + ((3, 4, 4, 80, 128),)
    + ((3, 4, 48, 128), (3, 48, 128), (3, 4, 32, 128), (3, 32, 128))
    + ((3, 80, 256),)
)
N_REDUCE = len(REDUCE_SHAPES)


def reduce_gen(wire, src, out, bufs, sem):
    total, rcore = bufs[0], bufs[1]
    plane, ring, late, from_y = (bufs[2:4], bufs[4:6]), bufs[6], (bufs[7:9], bufs[9:11]), bufs[11]
    x, z, c = place()
    y = lax.axis_index("dp")
    mine = row_split()[0]
    theirs = pl.ds(multiple(64 - 64 * c, 16), 80)
    hi, lo = pl.ds(256, 128), pl.ds(0, 256)
    load = pltpu.make_async_copy(src.at[:, :, :, mine], total, sem)
    load.start()

    def plane_first(h):
        ys = pl.ds(2 * h, 2)

        def view(f, s):
            xi, zi = xz(h, f, s)
            return total.at[xi, zi, ys, :, lo]

        def give(f):
            xi, zi = xz(h, f, ALL)
            return src.at[xi, zi, ys, theirs, lo]

        def dst(f):
            xi, zi = xz(h, f, ALL)
            return rcore.at[xi, zi, ys, :, lo]

        ready_of = core_swap(wire, halves(h)[1][0], give, dst)
        return scatter_half(wire, h, view, plane[h], ready_of(lambda f: view(f, ALL)))

    def y_first():
        def at(i):
            return total.at[:, :, i, :, hi]

        ready_of = core_swap(
            wire, y, lambda i: src.at[:, :, i, theirs, hi], lambda i: rcore.at[:, :, i, :, hi]
        )

        def after():
            yield from ring_reduce(wire, y, on_y, at, ring, ready_of(at))

            def half(h):
                rows = pl.ds(48 * h, 48 - 16 * h)

                def view(f, s):
                    xi, zi = xz(h, f, s)
                    return total.at[xi, zi, y, rows, hi]

                return scatter_half(wire, h, view, late[h], lambda d: None)

            yield from lockstep([half(0), half(1)])

        return after()

    gens = [plane_first(0), plane_first(1), y_first()]
    yield
    load.wait()
    yield from lockstep(gens)
    piece = total.at[x, z]
    yield from ring_reduce(
        wire, y, on_y, lambda i: piece.at[i, :, lo], from_y, lambda d: None
    )
    out[x, z, mine] = total[x, z, y]

    def spread(h):
        rows = pl.ds(multiple((96 * c, 48 + 16 * c)[h], 16), 48 - 16 * h)

        def view(f, s):
            xi, zi = xz(h, f, s)
            return out.at[xi, zi, rows]

        def share(f, s, core):
            xi, zi = xz(h, f, s)
            begin = multiple((96 * core, 48 + 32 * core)[h], 16)
            return out.at[xi, zi, pl.ds(begin, 48 - 32 * h)]

        return gather_half(wire, h, view, share)

    yield from lockstep([spread(0), spread(1)])


ATTN_REDUCE_SHAPES = (
    ((4, 4, 80, 384),) * 2
    + ((3, 4, 80, 384),)
    + ((3, 48, 384), (3, 48, 384), (3, 32, 384), (3, 32, 384), (48, 384), (32, 384))
)


def attn_reduce_gen(wire, src, out, bufs):
    total, rcore, ring = bufs[:3]
    one, two, held = (bufs[3], bufs[5]), (bufs[4], bufs[6]), bufs[7:9]
    c = place()[2]
    y = lax.axis_index("dp")
    oth = {"ctx": other_core()}
    mine = row_split()[0]
    theirs = pl.ds(multiple(64 - 64 * c, 16), 80)
    total[...] = src[:, :, mine]

    def at(i):
        return total.at[:, i]

    ready_of = core_swap(wire, y, lambda i: src.at[:, i, theirs], lambda i: rcore.at[:, i])
    yield from ring_reduce(wire, y, on_y, at, ring, ready_of(at))

    def half(h):
        axes, (me, _) = halves(h)
        rows = pl.ds(48 * h, 48 - 16 * h)
        where = pl.ds(multiple(64 * c + 48 * h, 16), 48 - 16 * h)
        yield from ring_reduce(
            wire, me, lambda d: on_plane(axes[0], d), lambda i: total.at[i, y, rows], one[h],
            lambda d: None,
        )
        base = wire.take(3)
        for j, d in enumerate(DIRS):
            wire.go(total.at[me, y, rows], two[h].at[j], base + j, on_plane(axes[1], d))
        yield
        for j, d in enumerate(DIRS):
            wire.got(two[h].at[j], base + j, oth)
        sums = total[me, y, rows].astype(F32)
        for j in range(3):
            sums = sums + two[h][j].astype(F32)
        held[h][...] = sums.astype(BF)
        base = wire.take(3)
        out[me, where] = held[h][...]
        for j, d in enumerate(DIRS):
            wire.go(held[h], out.at[me, where], base + j, on_plane(axes[0], d))
        yield
        for j, d in enumerate(DIRS):
            wire.got(out.at[turn(me, -d), where], base + j, oth)

    yield from lockstep([half(0), half(1)])
    base = wire.take(1)

    def handed(core):
        return out.at[:, pl.ds(multiple(80 * core, 16), 64)]

    wire.go(handed(c), handed(c), base, oth)
    yield
    wire.got(handed(1 - c), base, oth)


def gains_gen(wire, steps, got):
    y = lax.axis_index("dp")
    base = wire.take(10)
    k = 0
    for stage in range(4):
        if stage < 2:
            there = [(d, {"ctx": neighbour(stage, d)}) for d in (1, -1, 2)]
        elif stage == 2:
            there = [(0, {"ctx": other_core()})]
        else:
            there = [(d, {"dp": turn(y, d)}) for d in (1, 2, 3)]
        for i, (d, dev) in enumerate(there):
            wire.go(steps.at[stage], got.at[k + i], base + k + i, dev)
        yield
        total = steps[stage]
        for i, (d, dev) in enumerate(there):
            wire.got(got.at[k + i], base + k + i, dev)
            total = total + got[k + i]
        steps[stage + 1] = total
        k += len(there)


def pack_weights(wq, wk, wv, wo, wg, wu, wd):
    def blocks(w):
        return w.reshape(LAYERS, 144, 4, 384).transpose(0, 2, 1, 3)

    attn = blocks(jnp.concatenate([wk, wv, wq, wo], axis=2))
    gate, up = blocks(wg), blocks(wu)
    down = wd.transpose(0, 2, 1).reshape(LAYERS, 4, 144, 384)
    return (
        attn[0],
        jnp.stack([gate[0], up[0], attn[1], down[0]]),
        jnp.stack([gate[1], up[1], up[1], down[1]]),
    )


def unpack_grads(early, late, attn0):
    attn = jnp.stack([attn0, late[2]]).astype(F32)

    def cols(v):
        return v.transpose(0, 2, 1, 3).reshape(LAYERS, 144, 1536)

    def both(i):
        return jnp.stack([late[i], early[i]]).astype(F32)

    attn = cols(attn)
    down = both(3).reshape(LAYERS, D, 384).transpose(0, 2, 1)
    return (
        attn[:, :, 384:960], attn[:, :, :192], attn[:, :, 192:384], attn[:, :, 960:],
        cols(both(0)), cols(both(1)), down,
    )


def body(
    tokens, out_grad, w_query, w_key, w_value, w_out, w_gate, w_up, w_down_, attn_gain, ffn_gain,
    block_pairs,
):
    me = lax.axis_index("ctx")
    y = lax.axis_index("dp")
    mine = block_pairs[me]
    offs = jnp.arange(64, dtype=jnp.int32)
    pos = jnp.concatenate([mine * 64 + offs, (63 - mine) * 64 + offs])
    freq = ROPE_BASE ** (-2.0 * jnp.arange(HD // 2, dtype=F32) / HD)
    ang = pos.astype(F32)[:, None] * freq[None, :]
    cos = jnp.cos(ang)
    sin = jnp.sin(ang)
    cos = jnp.concatenate([cos] * 4, axis=1)
    ssin = jnp.concatenate([-sin, sin, -sin, sin], axis=1)
    is_lo = block_pairs < mine
    is_hi = block_pairs > mine
    scal = jnp.stack([
        jnp.where(is_lo, 0.0, NEG), jnp.where(is_hi, 0.0, NEG),
        jnp.where(is_lo, 1.0, 0.0), jnp.where(is_lo | is_hi, 0.0, BIG),
    ]).astype(F32)
    lane = jnp.arange(128)[None, :]
    lo_col = jnp.repeat(is_lo, 64)[:, None]
    hi_col = jnp.repeat(is_hi, 64)[:, None]
    mask = jnp.where(lane < 64, lo_col, hi_col).astype(BF).reshape(8, 256, 128)
    ind = ((lane == 64) | ((lane == 65) & lo_col) | ((lane == 66) & hi_col)).astype(BF)
    ind = ind.reshape(8, 256, 128)

    win_a, win_b, win_m = pack_weights(w_query, w_key, w_value, w_out, w_gate, w_up, w_down_)
    gin = jnp.zeros((16, 256), BF)
    gin = gin.at[0:2, :144].set(attn_gain).at[2:4, :144].set(ffn_gain)
    h = tokens.astype(F32)
    common = (cos, ssin, mask, ind, scal)
    out0 = first_forward(h, win_a, win_b, gin, *common)
    saved0, (w_a, w_b, gains) = out0[:7], out0[7:]
    out1 = second_forward(saved0[0], w_b, win_m, gains, *common)
    saved1, w_m = out1[:7], out1[7]
    result = saved1[0].astype(BF)
    g = out_grad.astype(F32)
    tail = (gains, cos, ssin, mask, scal)
    g, ga1, gg1, early = first_backward((g, saved0[0]) + saved1[1:] + tail + (w_b[2], w_m))
    g, late, attn0, gg = second_backward((g, h) + saved0[1:] + tail + (w_a, w_b), ga1, gg1)
    grads = unpack_grads(early, late, attn0)
    gg = lax.dynamic_slice(gg, (0, y * 144), (4, 144))
    return (result, g) + grads + (gg[0::2], gg[1::2])


def solution(mesh):
    row = P(("dp", "ctx"), None)
    mat = P(None, "dp", None)
    vec = P(None, "dp")
    return jax.shard_map(
        body,
        mesh=mesh,
        in_specs=(row, row) + (mat,) * 7 + (vec, vec, P()),
        out_specs=(row, row) + (mat,) * 7 + (vec, vec),
        check_vma=False,
    )
```

time: 417 us -> 347 us (0.83); the launches traced: 416 us -> 341 us
  blocking collectives: 64.2 us -> 0 us
  Pallas kernels: 314 us -> 303 us
    psum x1 -> x0, blocking collectives: 64.2 us -> none  [body(): ggs[l] = lax.psum(gg[:2], ('dp', 'ctx'))]
    pallas_call x6 -> x4, Pallas kernels: 314 us -> 303 us  [the longest x1 101 us: second_backward(): pl.pallas_call(second_backward_kernel, out_shape=(jax.ShapeDtypeStruct((1...]
where the time goes in v2:
time: 347 us; the launch traced here: 341 us
  Pallas kernels  303 us (87%)
  local copies, waits for them, and re-layouts  24.4 us (7%)
  other arithmetic  10.9 us (3%)
    pallas_call x1, Pallas kernels, second_backward(): pl.pallas_call(second_backward_kernel, out_shape=(jax.ShapeDtypeStruct((1...  101 us
    pallas_call x1, Pallas kernels, first_backward(): pl.pallas_call(first_backward_kernel, out_shape=(jax.ShapeDtypeStruct((12...  75.6 us
    pallas_call x1, Pallas kernels, first_forward(): pl.pallas_call(first_forward_kernel, out_shape=SAVED + (ATTN_GATHERED, GA...  74.3 us
    pallas_call x1, Pallas kernels, second_forward(): pl.pallas_call(second_forward_kernel, out_shape=SAVED + (GATHERED,), in_s...  52.2 us

profile of v2, /device:TPU:1, one launch (start us, length us, event | category | flops | bytes accessed | tf_op | source)
XLA Modules:
  0.0 340.9 jit_solution(15128978488313690032)
XLA Ops:
  0.7 1.3 dynamic_slice.6
  3.4 1.3 select_bitcast_fusion.2
  6.5 1.5 scatter.9.gin
  8.1 1.1 copy.37
  9.2 0.8 convert_element_type.29.h_ref.refs_1_
  11.8 1.8 copy.42.refs_0_
  14.2 0.9 fusion.9
  15.6 1.0 copy-done.3
  16.8 1.0 copy-done.4
  17.8 2.1 pad_maximum_fusion
  19.9 1.5 or_convert_fusion
  21.4 74.3 %first_forward.1 = (f32[128,576]{1,0:T(8,128)}, f32[128,576]{1,0:T(8,128)}, bf16[128,640]{1,0:T(8,128)(2,1)}, bf16[3,384,256]{2,1,0:T(8,128)(2,1)}, bf16[4,4,2,3...) custom-call(f32[128,576]{1,0:T(8,128)} %convert_element_type.29.h_re, ...), custom_call_target="tpu_custom_call" | custom-call | tf_op jit(solution)/shard_map/first_forward/pallas_call | solution.py:716
  95.7 2.9 slice_bitcast_fusion.refs_13_
  98.6 52.2 %second_forward.1 = (f32[128,576]{1,0:T(8,128)}, f32[128,576]{1,0:T(8,128)}, bf16[128,640]{1,0:T(8,128)(2,1)}, bf16[3,384,256]{2,1,0:T(8,128)(2,1)}, bf16[4,4,2,...) custom-call(f32[128,576]{1,0:T(8,128)} %get-tuple-element.61.h_ref.r, ...), custom_call_target="tpu_custom_call" | custom-call | tf_op jit(solution)/shard_map/second_forward/pallas_call | solution.py:731
  150.8 1.0 convert_element_type.33
  151.8 0.8 copy.46
  152.6 75.6 %first_backward.1 = (f32[128,576]{1,0:T(8,128)}, bf16[4,4,144,384]{3,2,1,0:T(8,128)(2,1)}, f32[8,576]{1,0:T(8,128)}, bf16[4,4,144,384]{3,2,1,0:T(8,128)(2,1)}) custom-call(f32[128,576]{1,0:T(8,128)} %copy.42.refs_0_, f32[128,576]{1,0:T(8,128)} %get-tuple-element.61.h_ref.refs_1_, f32[128,576]{1,0:T(8,128)} %get-tuple-element.65.refs_2_, ...), custom_call_target="tpu_custom_call" | custom-call | tf_op jit(solution)/shard_map/first_backward/pallas_call | solution.py:1020
  228.1 101.2 %second_backward.1 = (f32[128,576]{1,0:T(8,128)}, bf16[4,4,144,384]{3,2,1,0:T(8,128)(2,1)}, bf16[4,144,384]{2,1,0:T(8,128)(2,1)}, f32[8,640]{1,0:T(8,128)}) custom-call(f32[128,576]{1,0:T(8,128)} %get-tuple-element.72.refs_0_, f32[128,576]{1,0:T(8,128)} %convert_element_type.29.h_ref.refs_1_, f32[128,576]{1,0:T(8,128)} %get-tuple-element.73.refs_2_, ...), custom_call_target="tpu_custom_call" | custom-call | tf_op jit(solution)/shard_map/second_backward/pallas_call | solution.py:1046
  329.4 2.0 copy.47
  333.7 1.3 convert_bitcast_fusion.3
  335.1 1.4 copy.53
  336.7 1.4 copy.52
  338.5 0.9 fusion.5
  339.4 1.3 fusion.4
  (53 shorter events, 8.0 us)
Async XLA Ops:
  0.6 12.9 %copy-start.7 = (bf16[2,144,576]{2,1,0:T(8,128)(2,1)S(1)}, bf16[2,144,576]{2,1,0:T(8,128)(2,1)}, u32[]{:S(2)}) copy-start(bf16[2,144,576]{2,1,0:T(8,128)(2,1)} %param.21) | copy-start | bytes 995332
  0.7 12.9 %copy-start.9 = (bf16[2,144,192]{2,1,0:T(8,128)(2,1)S(1)}, bf16[2,144,192]{2,1,0:T(8,128)(2,1)}, u32[]{:S(2)}) copy-start(bf16[2,144,192]{2,1,0:T(8,128)(2,1)} %param.20) | copy-start | bytes 331780
  0.7 12.9 %copy-start.8 = (bf16[2,144,192]{2,1,0:T(8,128)(2,1)S(1)}, bf16[2,144,192]{2,1,0:T(8,128)(2,1)}, u32[]{:S(2)}) copy-start(bf16[2,144,192]{2,1,0:T(8,128)(2,1)} %param.19) | copy-start | bytes 331780
  0.7 12.9 %copy-start.6 = (bf16[2,144,576]{2,1,0:T(8,128)(2,1)S(1)}, bf16[2,144,576]{2,1,0:T(8,128)(2,1)}, u32[]{:S(2)}) copy-start(bf16[2,144,576]{2,1,0:T(8,128)(2,1)} %param.18) | copy-start | bytes 995332
  8.1 6.0 %copy-start.10 = (bf16[16,256]{1,0:T(8,128)(2,1)}, bf16[16,256]{1,0:T(8,128)(2,1)S(1)}, u32[]{:S(2)}) copy-start(bf16[16,256]{1,0:T(8,128)(2,1)S(1)} %scatter.9.gin) | copy-start | bytes 24580
  14.1 1.3 copy-start.2
  15.4 1.2 copy-start.3
  16.6 1.2 copy-start.4
  228.1 105.2 %copy-start.1 = (bf16[4,4,144,384]{3,2,1,0:T(8,128)(2,1)S(1)}, bf16[4,4,144,384]{3,2,1,0:T(8,128)(2,1)}, u32[]{:S(2)}) copy-start(bf16[4,4,144,384]{3,2,1,0:T(8,128)(2,1)} %get-tuple-element.85) | copy-start | bytes 5308420
  329.4 4.1 %copy-start = (bf16[4,4,144,384]{3,2,1,0:T(8,128)(2,1)S(1)}, bf16[4,4,144,384]{3,2,1,0:T(8,128)(2,1)}, u32[]{:S(2)}) copy-start(bf16[4,4,144,384]{3,2,1,0:T(8,128)(2,1)} %get-tuple-element.84) | copy-start | bytes 5308420
  336.7 1.4 copy-start.5
